TPU v7x, 128 devices: a whole 4x4x4 slice. The times are simulated.
128 devices in a mesh: row: 16 (over x, y), col: 8 (over z, core).
Axes of the slice: x: 4, y: 4, z: 4, core: 2. Of those that a mesh axis runs over, the one named last changes fastest.
Arguments:
- inputs: bfloat16 [512, 12288], P('col', 'row'), may hold values from -6 to 6
- w_up: bfloat16 [12288, 24576], P('row', 'col'), may hold values from -0.0546875 to 0.0546875
- w_down: bfloat16 [24576, 12288], P('col', 'row'), may hold values from -0.0390625 to 0.0390625
- mask_up: int32 [96, 192], P('row', 'col'), may hold values from 0 to 1, as said below
- mask_down: int32 [192, 96], P('col', 'row'), may hold values from 0 to 1, as said below
- cotangent: bfloat16 [512, 12288], P('col', 'row'), may hold values from -1.5 to 1.5
Outputs:
- outputs: bfloat16 [512, 12288], P('col', 'row')
- grad_inputs: bfloat16 [512, 12288], P('col', 'row')
- grad_up: bfloat16 [12288, 24576], P('row', 'col')
- grad_down: bfloat16 [24576, 12288], P('col', 'row')
Inputs may be any that keep to these rules, and one draw needn't show every extreme that they name: `mask_up`: each entry is 0 or 1; the chance of a 1 is the same along a row of tiles and differs from row to row, between 0.2 and 0.8. `mask_down`: each entry is 0 or 1; the chance of a 1 is the same along a row of tiles and differs from row to row, between 0.2 and 0.8.
All inputs are finite; a program needn't handle non-finite values.
Results may differ from a plain program's by a relative error of at most 0.029.
Values may be sent and summed in bfloat16 or wider, within the bound.
A program may use at most 128 MiB of HBM per device.

v0:
```python
import jax
import jax.numpy as jnp
from jax import lax
from jax.sharding import PartitionSpec as P


def apply_mask(weight, mask):
    rows, cols = mask.shape
    tile = weight.shape[0] // rows
    shaped = weight.reshape(rows, tile, cols, tile)
    keep = mask[:, None, :, None].astype(weight.dtype)
    return (shaped * keep).reshape(weight.shape)


def smooth_gate(value):
    return jax.nn.gelu(value, approximate=True)


def activate(hidden, grad_act):
    act = smooth_gate(hidden).astype(jnp.bfloat16)
    _, pull = jax.vjp(smooth_gate, hidden)
    grad_hidden = pull(grad_act)[0].astype(jnp.bfloat16)
    return (act, grad_hidden)


def contract(left, right, left_dim, right_dim):
    return lax.dot_general(
        left, right, (((left_dim,), (right_dim,)), ((), ())), preferred_element_type=jnp.float32
    )


def per_device(inputs, w_up, w_down, mask_up, mask_down, cotangent):
    up_kept = apply_mask(w_up, mask_up)
    down_kept = apply_mask(w_down, mask_down)
    inputs_all, cot_all = (
        lax.all_gather(inputs, "col", axis=0, tiled=True),
        lax.all_gather(cotangent, "col", axis=0, tiled=True),
    )
    up_part = jnp.dot(inputs_all, up_kept, preferred_element_type=jnp.float32)
    back_part = contract(cot_all, down_kept, 1, 1)
    hidden, grad_act = (
        lax.psum_scatter(
            up_part.astype(jnp.bfloat16), "row", scatter_dimension=0, tiled=True
        ).astype(jnp.float32),
        lax.psum_scatter(
            back_part.astype(jnp.bfloat16), "row", scatter_dimension=0, tiled=True
        ).astype(jnp.float32),
    )
    act, grad_hidden = activate(hidden, grad_act)
    act_all, grad_all = (
        lax.all_gather(act, "row", axis=0, tiled=True),
        lax.all_gather(grad_hidden, "row", axis=0, tiled=True),
    )
    out_part = jnp.dot(act_all, down_kept, preferred_element_type=jnp.float32)
    input_part = contract(grad_all, up_kept, 1, 1)
    outputs, grad_inputs = (
        lax.psum_scatter(
            out_part.astype(jnp.bfloat16), "col", scatter_dimension=0, tiled=True
        ).astype(jnp.float32),
        lax.psum_scatter(
            input_part.astype(jnp.bfloat16), "col", scatter_dimension=0, tiled=True
        ).astype(jnp.float32),
    )
    grad_down = apply_mask(contract(act_all, cot_all, 0, 0).astype(jnp.bfloat16), mask_down)
    grad_up = apply_mask(contract(inputs_all, grad_all, 0, 0).astype(jnp.bfloat16), mask_up)
    return (outputs.astype(jnp.bfloat16), grad_inputs.astype(jnp.bfloat16), grad_up, grad_down)


def solution(mesh):
    in_specs = (
        P("col", "row"),
        P("row", "col"),
        P("col", "row"),
        P("row", "col"),
        P("col", "row"),
        P("col", "row"),
    )
    out_specs = (P("col", "row"), P("col", "row"), P("row", "col"), P("col", "row"))
    return jax.shard_map(
        per_device, mesh=mesh, in_specs=in_specs, out_specs=out_specs, check_vma=False
    )
```

profile of v0, /device:TPU:1, one launch (start us, length us, event | category | flops | bytes accessed | tf_op | source)
XLA Modules:
  0.0 366.4 jit_solution(9498156294956515062)
XLA Ops:
  7.2 0.0 reduce-scatter.15.cloned.1.call-start
  7.2 17.2 %all_gather.14 = bf16[512,768]{1,0:T(8,128)(2,1)} all-gather(bf16[64,768]{1,0:T(8,128)(2,1)} %param.11), channel_id=1, replica_groups=mesh['row'=16,'col'=8] {'col'}, dimensions={0}, use_global_device_ids=true | all-gather | bytes 884736 | tf_op jit(solution)/shard_map/all_gather | solution.py:37
  24.4 0.0 copy-start.7
  24.4 6.6 %copy.25 = bf16[3072,768]{0,1:T(8,128)(2,1)} copy(bf16[3072,768]{1,0:T(8,128)(2,1)} %param.8) | data formatting | bytes 9437184 | tf_op args[2]
  31.1 0.0 copy-done.7
  31.1 0.0 copy-start.2
  31.1 0.7 mul.90
  31.7 0.0 copy-start
  31.8 2.4 copy-done
  34.2 0.9 copy-done.2
  35.1 4.5 %fusion.2 = bf16[512,3072]{0,1:T(8,128)(2,1)S(1)} fusion(bf16[512,768]{1,0:T(8,128)(2,1)} %all_gather.14, bf16[3072,768]{0,1:T(8,128)(2,1)S(1)} %copy-done.2, bf16[96,8,24,128]{3,2,1,0:T(8,128)(2,1)S(1)} %bitcast.38), kind=kOutput, calls=%fused_computation.9 | convolution fusion | flops 2419851264 | bytes 13369344 | tf_op jit(solution)/shard_map/dot_general | solution.py:27
  39.6 0.0 copy-start.8
  39.6 0.0 copy-start.6
  39.6 3.1 copy.32
  42.7 0.0 reduce-scatter.15.cloned.1.call-update
  42.7 0.0 reduce-scatter.13.cloned.1.call-start
  42.7 0.0 copy-done.8
  42.8 0.0 copy-done.6
  42.8 13.4 %all_gather.12 = bf16[512,768]{1,0:T(8,128)(2,1)S(1)} all-gather(bf16[64,768]{1,0:T(8,128)(2,1)S(1)} %copy-done.6), channel_id=1, replica_groups=mesh['row'=16,'col'=8] {'col'}, dimensions={0}, use_global_device_ids=true | all-gather | bytes 884736 | tf_op jit(solution)/shard_map/all_gather | solution.py:36
  56.1 0.0 copy-start.4
  56.1 0.7 mul.83
  56.8 0.0 copy-start.1
  56.8 0.2 copy-done.4
  57.0 1.9 copy-done.1
  59.0 5.1 %fusion.1 = bf16[512,3072]{0,1:T(8,128)(2,1)S(1)} fusion(bf16[512,768]{1,0:T(8,128)(2,1)S(1)} %all_gather.12, bf16[768,3072]{1,0:T(8,128)(2,1)} %param.7, bf16[96,8,24,128]{3,2,1,0:T(8,128)(2,1)S(1)} %bitcast.41), kind=kOutput, calls=%fused_computation.8 | convolution fusion | flops 2419851264 | bytes 13369344 | tf_op jit(solution)/shard_map/dot_general | solution.py:39
  64.1 3.1 copy.30
  67.2 0.0 reduce-scatter.13.cloned.1.call-update
  67.2 0.0 all-gather.3.cloned.1.call-start
  67.2 50.3 %reduce-scatter.15.cloned.1.call-done = bf16[32,3072]{1,0:T(8,128)(2,1)} async-done(((bf16[512,3072]{1,0:T(8,128)(2,1)}), bf16[32,3072]{1,0:T(8,128)(2,1)}) %reduce-scatter.15.cloned.1.call-update) | async-done | bytes 196624 | tf_op jit(solution)/shard_map/reduce_scatter | solution.py:45
  117.6 78.4 %reduce-scatter.13.cloned.1.call-done = bf16[32,3072]{1,0:T(8,128)(2,1)} async-done(((bf16[512,3072]{1,0:T(8,128)(2,1)}), bf16[32,3072]{1,0:T(8,128)(2,1)}) %reduce-scatter.13.cloned.1.call-update) | async-done | bytes 196624 | tf_op jit(solution)/shard_map/reduce_scatter | solution.py:42
  195.9 2.1 fusion.12
  198.0 0.0 all-gather.3.cloned.1.call-update
  198.0 0.0 all-gather.5.cloned.1.call-start
  198.1 0.5 all-gather.5.cloned.1.call-update
  198.6 0.0 reduce-scatter.9.cloned.1.call-start
  198.7 48.0 %all-gather.3.cloned.1.call-done = bf16[512,3072]{1,0:T(8,128)(2,1)} async-done(((bf16[32,3072]{1,0:T(8,128)(2,1)}), bf16[512,3072]{1,0:T(8,128)(2,1)}) %all-gather.3.cloned.1.call-update) | async-done | bytes 3145744 | tf_op jit(solution)/shard_map/all_gather | solution.py:51
  246.7 8.2 %fusion.6 = bf16[512,768]{1,0:T(8,128)(2,1)} fusion(bf16[512,3072]{1,0:T(8,128)(2,1)} %all-gather.3.cloned.1.call-done, bf16[3072,768]{0,1:T(8,128)(2,1)} %copy.25, bf16[96,8,24,128]{3,2,1,0:T(8,128)(2,1)} %bitcast.39), kind=kOutput, calls=%fused_computation.13 | convolution fusion | flops 2418671616 | bytes 13369344 | tf_op jit(solution)/shard_map/dot_general | solution.py:54
  254.9 0.0 reduce-scatter.9.cloned.1.call-update
  254.9 0.2 reduce-scatter.11.cloned.1.call-start
  255.1 40.4 %all-gather.5.cloned.1.call-done = bf16[512,3072]{1,0:T(8,128)(2,1)} async-done(((bf16[32,3072]{1,0:T(8,128)(2,1)}), bf16[512,3072]{1,0:T(8,128)(2,1)}) %all-gather.5.cloned.1.call-update) | async-done | bytes 3145744 | tf_op jit(solution)/shard_map/all_gather | solution.py:52
  295.5 8.2 %convolution_convert_fusion.4 = bf16[512,768]{1,0:T(8,128)(2,1)} fusion(bf16[512,3072]{1,0:T(8,128)(2,1)} %all-gather.5.cloned.1.call-done, bf16[768,3072]{1,0:T(8,128)(2,1)} %param.7, bf16[96,8,24,128]{3,2,1,0:T(8,128)(2,1)} %bitcast.42), kind=kOutput, calls=%fused_computation.14 | convolution fusion | flops 2418671616 | bytes 13369344 | tf_op jit(solution)/shard_map/dot_general | solution.py:27
  303.7 0.0 reduce-scatter.11.cloned.1.call-update
  303.7 5.9 %copy.49 = bf16[96,8,24,128]{3,1,2,0:T(8,128)(2,1)} copy(bf16[96,8,24,128]{3,2,1,0:T(8,128)(2,1)} %bitcast.43) | data formatting | bytes 9437184
  309.7 5.9 %copy.48 = bf16[96,8,24,128]{3,1,2,0:T(8,128)(2,1)} copy(bf16[96,8,24,128]{3,2,1,0:T(8,128)(2,1)} %bitcast.40) | data formatting | bytes 9437184
  315.6 6.6 %copy.27 = bf16[768,3072]{0,1:T(8,128)(2,1)} copy(bf16[768,3072]{1,0:T(8,128)(2,1)} %bitcast.44) | data formatting | bytes 9437184 | tf_op jit(solution)/shard_map/mul | solution.py:12
  322.2 0.0 copy-start.5
  322.2 6.7 %copy.28 = bf16[3072,768]{1,0:T(8,128)(2,1)} copy(bf16[3072,768]{0,1:T(8,128)(2,1)} %bitcast.45) | data formatting | bytes 9437184 | tf_op jit(solution)/shard_map/mul | solution.py:12
  328.9 0.0 copy-done.5
  328.9 8.1 %bitcast_multiply_fusion = bf16[768,3072]{0,1:T(8,128)(2,1)} fusion(bf16[768,3072]{0,1:T(8,128)(2,1)} %copy.27, bf16[512,3072]{1,0:T(8,128)(2,1)} %all-gather.5.cloned.1.call-done, bf16[512,768]{1,0:T(8,128)(2,1)S(1)} %copy-done.5), kind=kOutput, calls=%fused_computation.4 | convolution fusion | flops 2420637696 | bytes 13369344 | tf_op jit(solution)/shard_map/dot_general | solution.py:27
  337.1 0.0 copy-start.3
  337.1 6.7 %copy.29 = bf16[768,3072]{1,0:T(8,128)(2,1)} copy(bf16[768,3072]{0,1:T(8,128)(2,1)} %bitcast_multiply_fusion) | data formatting | bytes 9437184
  343.8 0.0 copy-done.3
  343.8 8.2 %fusion = bf16[3072,768]{1,0:T(8,128)(2,1)} fusion(bf16[3072,768]{1,0:T(8,128)(2,1)} %copy.28, bf16[512,3072]{1,0:T(8,128)(2,1)} %all-gather.3.cloned.1.call-done, bf16[512,768]{1,0:T(8,128)(2,1)S(1)} %copy-done.3), kind=kOutput, calls=%fused_computation.5 | convolution fusion | flops 2420637696 | bytes 13369344 | tf_op jit(solution)/shard_map/dot_general | solution.py:27
  352.0 0.0 reduce-scatter.9.cloned.1.call-done
  352.0 7.5 %reduce-scatter.11.cloned.1.call-done = bf16[64,768]{1,0:T(8,128)(2,1)} async-done(((bf16[512,768]{1,0:T(8,128)(2,1)}), bf16[64,768]{1,0:T(8,128)(2,1)}) %reduce-scatter.11.cloned.1.call-update) | async-done | bytes 98320 | tf_op jit(solution)/shard_map/reduce_scatter | solution.py:60
  (2 shorter events, 0.0 us)
Async XLA Ops:
  7.2 110.4 %reduce-scatter.15.cloned.1.call-start = ((), (), s32[]{:S(2)}) async-start(), calls=%async_computation.9 | async-start | bytes 3342336 | tf_op jit(solution)/shard_map/reduce_scatter | solution.py:45
  24.4 6.6 %copy-start.7 = (s32[24,6]{0,1:T(8,128)S(1)}, s32[24,6]{0,1:T(8,128)}, u32[]{:S(2)}) copy-start(s32[24,6]{0,1:T(8,128)} %param.10) | copy-start | bytes 1732
  31.1 4.0 %copy-start.2 = (bf16[3072,768]{0,1:T(8,128)(2,1)S(1)}, bf16[3072,768]{0,1:T(8,128)(2,1)}, u32[]{:S(2)}) copy-start(bf16[3072,768]{0,1:T(8,128)(2,1)} %copy.25) | copy-start | bytes 14155780
  31.7 2.4 copy-start
  39.6 3.2 copy-start.8
  39.6 3.2 copy-start.6
  42.7 153.2 %reduce-scatter.13.cloned.1.call-start = ((), (), s32[]{:S(2)}) async-start(), calls=%async_computation.8 | async-start | bytes 3342336 | tf_op jit(solution)/shard_map/reduce_scatter | solution.py:42
  56.1 0.9 copy-start.4
  56.8 2.1 copy-start.1
  67.2 179.5 %all-gather.3.cloned.1.call-start = ((), (), s32[]{:S(2)}) async-start(), calls=%async_computation.4 | async-start | bytes 3342336 | tf_op jit(solution)/shard_map/all_gather | solution.py:51
  198.0 97.5 %all-gather.5.cloned.1.call-start = ((), (), s32[]{:S(2)}) async-start(), calls=%async_computation.6 | async-start | bytes 3342336 | tf_op jit(solution)/shard_map/all_gather | solution.py:52
  198.6 153.4 %reduce-scatter.9.cloned.1.call-start = ((), (), s32[]{:S(2)}) async-start(), calls=%async_computation.5 | async-start | bytes 884736 | tf_op jit(solution)/shard_map/reduce_scatter | solution.py:57
  254.9 104.6 %reduce-scatter.11.cloned.1.call-start = ((), (), s32[]{:S(2)}) async-start(), calls=%async_computation.7 | async-start | bytes 884736 | tf_op jit(solution)/shard_map/reduce_scatter | solution.py:60
  322.2 6.7 %copy-start.5 = (bf16[512,768]{1,0:T(8,128)(2,1)S(1)}, bf16[512,768]{1,0:T(8,128)(2,1)}, u32[]{:S(2)}) copy-start(bf16[512,768]{1,0:T(8,128)(2,1)} %copy-done.4) | copy-start | bytes 2359300
  337.1 6.7 %copy-start.3 = (bf16[512,768]{1,0:T(8,128)(2,1)S(1)}, bf16[512,768]{1,0:T(8,128)(2,1)}, u32[]{:S(2)}) copy-start(bf16[512,768]{1,0:T(8,128)(2,1)} %all_gather.14) | copy-start | bytes 2359300
Sparse Core Ops, SparseCore 0:
  42.8 74.7 reduce-scatter.14
  120.9 74.9 reduce-scatter.12
  198.2 48.4 all-gather.2
  248.7 46.7 all-gather.4
  298.3 27.8 reduce-scatter.8
  329.2 30.2 reduce-scatter.10
where the time goes:
time: 369 us; the launch traced here: 366 us
  waiting for transfers between devices  225 us (61%)
  local copies, waits for them, and re-layouts  51.5 us (14%)
  matrix products  42.3 us (11%)
  blocking collectives  30.6 us (8%)
  between operations  14.2 us (4%)
    reduce_scatter x1, waiting for transfers between devices, per_device(): lax.psum_scatter(up_part.astype(jnp.bfloat16), 'row', scatter_dimension=0...  78.4 us
    reduce_scatter x1, waiting for transfers between devices, per_device(): lax.psum_scatter(back_part.astype(jnp.bfloat16), 'row', scatter_dimension...  50.3 us
    all_gather x1, waiting for transfers between devices, per_device(): lax.all_gather(act, 'row', axis=0, tiled=True)  48 us
    all_gather x1, waiting for transfers between devices, per_device(): lax.all_gather(grad_hidden, 'row', axis=0, tiled=True)  40.4 us
    unnamed x24, local copies, waits for them, and re-layouts  36.8 us
    dot_general x4, matrix products, contract(): lax.dot_general(left, right, (((left_dim,), (right_dim,)), ((), ())), pre...  29 us
    all_gather x1, blocking collectives, per_device(): lax.all_gather(cotangent, 'col', axis=0, tiled=True)  17.2 us
    mul x4, local copies, waits for them, and re-layouts, apply_mask(): return (shaped * keep).reshape(weight.shape)  14.7 us
  transfers between devices with their start and end apart: 6, of which 5 were waited for; matrix products, arithmetic and copies ran while one was open for 20% of the time, Pallas kernels for 0%

commit v1 on v0

v1 whole, which is shorter than its diff:
```python
import functools

import jax
import jax.numpy as jnp
from jax import lax
from jax.experimental import pallas as pl
from jax.experimental.pallas import tpu as pltpu
from jax.sharding import PartitionSpec as P

MESH = pl.DeviceIdType.MESH
BF16 = jnp.bfloat16
F32 = jnp.float32
SIDE = 4
CHUNKS = 4
COLS = 8
ROWS = 16
TOK = COLS * ROWS
BLK = TOK // SIDE
FEAT = 768
QW = 768
TILE = 128
SUB = FEAT // TILE
S0, S1, S2, S3, S4, S5, S6, S7, SEMS = 0, 7, 11, 15, 21, 27, 31, 35, 42

ORDER = (
    (0, 0), (0, 1), (1, 0), (0, 2), (1, 1), (0, 3), (2, 0), (1, 2), (2, 1), (1, 3), (3, 0), (2, 2), (3, 1), (2, 3),
    (4, 0), (3, 2), (4, 1), (3, 3), (5, 0), (4, 2), (5, 1), (4, 3), (6, 0), (5, 2), (6, 1), (5, 3), (6, 2), (6, 3),
    (7, 0), (7, 1), (7, 2), (7, 3),
)


def dot(left, right, right_dim):
    return lax.dot_general(left, right, (((1,), (right_dim,)), ((), ())), preferred_element_type=F32)


def block_kernel(
    inputs, w_up, w_down, mask_up, mask_down, cotangent,
    outputs, grad_inputs, x_out, act_out, grad_out,
    xin, up, down, ph, pg, r1h, r1g, r2h, r2g, sh, sg, r3h, r3g, act, grad, po, r7,
    send, recv, wsem, lsem,
):
    row, col = lax.axis_index("row"), lax.axis_index("col")
    x, y = row // SIDE, lax.rem(row, SIDE)

    def turn(v, by):
        return lax.rem(v + by, SIDE)

    def at_x(by):
        return (turn(x, by) * SIDE + y, col)

    def at_y(by):
        return (x * SIDE + turn(y, by), col)

    def col_of(by):
        return lax.rem(col + by, COLS)

    barrier = pltpu.get_barrier_semaphore()
    partners = [at_x(j) for j in (1, 2, 3)] + [at_y(j) for j in (1, 2, 3)] + [(row, col_of(j)) for j in range(1, COLS)]
    for device in partners:
        pl.semaphore_signal(barrier, inc=1, device_id=device, device_id_type=MESH)

    own = [
        pltpu.make_async_copy(inputs, xin.at[:, col, 0], lsem.at[0]),
        pltpu.make_async_copy(cotangent, xin.at[:, col, 1], lsem.at[1]),
    ]
    for copy in own:
        copy.start()
    loads = []
    for q in range(SIDE):
        loads.append(
            (
                pltpu.make_async_copy(w_up.at[:, pl.ds(q * QW, QW)], up.at[q], wsem.at[0, q]),
                pltpu.make_async_copy(w_down.at[pl.ds(q * QW, QW)], down.at[q], wsem.at[1, q]),
            )
        )
    for pair in loads:
        for copy in pair:
            copy.start()
    for copy in own:
        copy.wait()
    pl.semaphore_wait(barrier, len(partners))

    copies = {}

    def ship(c, slot, src, dst, device):
        copy = pltpu.make_async_remote_copy(
            src_ref=src,
            dst_ref=dst,
            send_sem=send.at[c, slot],
            recv_sem=recv.at[c, slot],
            device_id=device,
            device_id_type=MESH,
        )
        copy.start()
        copies[c, slot] = copy

    def land(c, first, last):
        for slot in range(first, last):
            copies[c, slot].wait_recv()

    for c in range(CHUNKS):
        for j in range(1, COLS):
            ship(c, S0 + j - 1, xin.at[c, col], xin.at[c, col], (row, col_of(j)))

    def drop_tiles(q, _):
        def one_row(i, _):
            rows = pl.ds(pl.multiple_of(i * TILE, TILE), TILE)
            for j in range(SUB):
                cols = pl.ds(j * TILE, TILE)
                up[q, rows, cols] = up[q, rows, cols] * mask_up[i, q * SUB + j].astype(F32).astype(BF16)
                down[q, rows, cols] = down[q, rows, cols] * mask_down[q * SUB + i, j].astype(F32).astype(BF16)
            return 0

        return lax.fori_loop(0, SUB, one_row, 0)

    for q in range(SIDE):
        for copy in loads[q]:
            copy.wait()
        drop_tiles(q, 0)

    def multiply_in(c):
        land(c, S0, S1)

        def part(q, _):
            ins = xin[c, :, 0].reshape(TOK, FEAT)
            ph[c, :, q] = dot(ins, up[q], 0).astype(BF16).reshape(SIDE, BLK, QW)
            cot = xin[c, :, 1].reshape(TOK, FEAT)
            pg[c, q] = dot(cot, down[q], 1).astype(BF16).reshape(SIDE, BLK, QW)
            return 0

        lax.fori_loop(0, SIDE, part, 0)
        ship(c, S1, ph.at[c, turn(x, 2), pl.ds(0, 2)], r1h.at[c, 0], at_x(1))
        ship(c, S1 + 1, pg.at[c, turn(y, 2), pl.ds(0, 2)], r1g.at[c, 0], at_y(1))
        ship(c, S1 + 2, ph.at[c, turn(x, 2), pl.ds(2, 2)], r1h.at[c, 1], at_x(3))
        ship(c, S1 + 3, pg.at[c, turn(y, 2), pl.ds(2, 2)], r1g.at[c, 1], at_y(3))

    def add_first(c):
        land(c, S1, S2)

        def half(k, _):
            ph[c, turn(x, 1), k] += r1h[c, 0, k]
            pg[c, turn(y, 1), k] += r1g[c, 0, k]
            ph[c, turn(x, 3), 2 + k] += r1h[c, 1, k]
            pg[c, turn(y, 3), 2 + k] += r1g[c, 1, k]
            return 0

        lax.fori_loop(0, 2, half, 0)
        ship(c, S2, ph.at[c, turn(x, 1)], r2h.at[c, 0], at_x(1))
        ship(c, S2 + 1, pg.at[c, turn(y, 1)], r2g.at[c, 0], at_y(1))
        ship(c, S2 + 2, ph.at[c, turn(x, 3)], r2h.at[c, 1], at_x(3))
        ship(c, S2 + 3, pg.at[c, turn(y, 3)], r2g.at[c, 1], at_y(3))

    def add_second(c):
        land(c, S2, S3)

        def quarter(k, _):
            for own_part, come, total, at in ((ph, r2h, sh, x), (pg, r2g, sg, y)):
                total[c, k] = (
                    own_part[c, at, k].astype(F32) + come[c, 0, k].astype(F32) + come[c, 1, k].astype(F32)
                ).astype(BF16)
            return 0

        lax.fori_loop(0, SIDE, quarter, 0)
        for j in (1, 2, 3):
            ship(c, S3 + 2 * (j - 1), sh.at[c, turn(y, j)], r3h.at[c, j - 1], at_y(j))
            ship(c, S3 + 2 * (j - 1) + 1, sg.at[c, turn(x, j)], r3g.at[c, j - 1], at_x(j))

    def activate(c):
        land(c, S3, S4)

        def some_rows(i, _):
            rows = pl.ds(pl.multiple_of(i * ROWS, ROWS), ROWS)
            value, slope = sh[c, y, rows].astype(F32), sg[c, x, rows].astype(F32)
            for j in range(3):
                value += r3h[c, j, rows].astype(F32)
                slope += r3g[c, j, rows].astype(F32)
            root = 0.7978845608028654
            square = value * value
            tan = jnp.tanh(root * (value + 0.044715 * (square * value)))
            gate = 0.5 * (1.0 + tan)
            bend = 0.5 * value * (1.0 - tan * tan) * (root * (1.0 + 3.0 * 0.044715 * square))
            act[c, x, y, rows] = (value * gate).astype(BF16)
            grad[c, y, x, rows] = (slope * (gate + bend)).astype(BF16)
            return 0

        lax.fori_loop(0, BLK // ROWS, some_rows, 0)
        for j in (1, 2, 3):
            ship(c, S4 + 2 * (j - 1), act.at[c, x, y], act.at[c, x, y], at_y(j))
            ship(c, S4 + 2 * (j - 1) + 1, grad.at[c, y, x], grad.at[c, y, x], at_x(j))

    def spread_first(c):
        land(c, S4, S5)
        ship(c, S5, act.at[c, x], act.at[c, x], at_x(1))
        ship(c, S5 + 1, grad.at[c, y], grad.at[c, y], at_y(1))
        ship(c, S5 + 2, act.at[c, x], act.at[c, x], at_x(3))
        ship(c, S5 + 3, grad.at[c, y], grad.at[c, y], at_y(3))

    def spread_second(c):
        land(c, S5, S6)
        low, high = pl.ds(0, 2), pl.ds(2, 2)
        left, right, under, over = turn(x, 3), turn(x, 1), turn(y, 3), turn(y, 1)
        ship(c, S6, act.at[c, left, low], act.at[c, left, low], at_x(1))
        ship(c, S6 + 1, grad.at[c, under, low], grad.at[c, under, low], at_y(1))
        ship(c, S6 + 2, act.at[c, right, high], act.at[c, right, high], at_x(3))
        ship(c, S6 + 3, grad.at[c, over, high], grad.at[c, over, high], at_y(3))

    held = []

    def multiply_out(c):
        land(c, S6, S7)
        for k, (src, dst) in enumerate(((act, act_out), (grad, grad_out))):
            copy = pltpu.make_async_copy(src.at[c], dst.at[c], lsem.at[2 + 2 * c + k])
            copy.start()
            held.append(copy)

        def part(n, _):
            cols = pl.ds(pl.multiple_of(n * 256, 256), 256)
            out = jnp.zeros((TOK, 256), F32)
            gin = jnp.zeros((TOK, 256), F32)
            for q in range(SIDE):
                out += dot(act[c, :, q].reshape(TOK, QW), down[q, :, cols], 0)
                gin += dot(grad[c, q].reshape(TOK, QW), up[q, cols], 1)
            po[c, :, 0, :, cols] = out.astype(BF16).reshape(COLS, ROWS, 256)
            po[c, :, 1, :, cols] = gin.astype(BF16).reshape(COLS, ROWS, 256)
            return 0

        lax.fori_loop(0, FEAT // 256, part, 0)
        for j in range(1, COLS):
            ship(c, S7 + j - 1, po.at[c, col_of(j)], r7.at[c, j - 1], (row, col_of(j)))

    def finish(c):
        land(c, S7, SEMS)
        for k, out in enumerate((outputs, grad_inputs)):
            total = po[c, col, k].astype(F32)
            for j in range(COLS - 1):
                total += r7[c, j, k].astype(F32)
            out[c] = total.astype(BF16)

    stages = (multiply_in, add_first, add_second, activate, spread_first, spread_second, multiply_out, finish)
    for stage, c in ORDER:
        stages[stage](c)
        if (stage, c) == (0, CHUNKS - 1):
            copy = pltpu.make_async_copy(xin, x_out, lsem.at[0])
            copy.start()
            held.append(copy)
    for copy in held:
        copy.wait()
    for copy in copies.values():
        copy.wait_send()


def run_block(inputs, w_up, w_down, mask_up, mask_down, cotangent):
    vmem = pl.BlockSpec(memory_space=pltpu.VMEM)
    smem = pl.BlockSpec(memory_space=pltpu.SMEM)
    hbm = pl.BlockSpec(memory_space=pl.ANY)
    piece = (BLK, QW)

    def buf(*dims):
        return pltpu.VMEM((CHUNKS, *dims), BF16)

    return pl.pallas_call(
        block_kernel,
        out_shape=[
            jax.ShapeDtypeStruct((CHUNKS, ROWS, FEAT), BF16),
            jax.ShapeDtypeStruct((CHUNKS, ROWS, FEAT), BF16),
            jax.ShapeDtypeStruct((CHUNKS, COLS, 2, ROWS, FEAT), BF16),
            jax.ShapeDtypeStruct((CHUNKS, SIDE, SIDE, *piece), BF16),
            jax.ShapeDtypeStruct((CHUNKS, SIDE, SIDE, *piece), BF16),
        ],
        in_specs=[hbm, hbm, hbm, smem, smem, hbm],
        out_specs=[vmem, vmem, hbm, hbm, hbm],
        scratch_shapes=[
            buf(COLS, 2, ROWS, FEAT),
            pltpu.VMEM((SIDE, FEAT, QW), BF16),
            pltpu.VMEM((SIDE, QW, FEAT), BF16),
            buf(SIDE, SIDE, *piece),
            buf(SIDE, SIDE, *piece),
            buf(2, 2, *piece),
            buf(2, 2, *piece),
            buf(2, SIDE, *piece),
            buf(2, SIDE, *piece),
            buf(SIDE, *piece),
            buf(SIDE, *piece),
            buf(3, *piece),
            buf(3, *piece),
            buf(SIDE, SIDE, *piece),
            buf(SIDE, SIDE, *piece),
            buf(COLS, 2, ROWS, FEAT),
            buf(COLS - 1, 2, ROWS, FEAT),
            pltpu.SemaphoreType.DMA((CHUNKS, SEMS)),
            pltpu.SemaphoreType.DMA((CHUNKS, SEMS)),
            pltpu.SemaphoreType.DMA((2, SIDE)),
            pltpu.SemaphoreType.DMA((2 + 2 * CHUNKS,)),
        ],
        compiler_params=pltpu.CompilerParams(
            collective_id=0, has_side_effects=True, vmem_limit_bytes=56 * 2**20
        ),
    )(
        inputs.reshape(CHUNKS, ROWS, FEAT),
        w_up,
        w_down,
        mask_up,
        mask_down,
        cotangent.reshape(CHUNKS, ROWS, FEAT),
    )


def weight_kernel(x_ref, act_ref, grad_ref, mask_up, mask_down, gup, gdown):
    q = pl.program_id(0)
    tokens = CHUNKS * TOK
    ins = x_ref[:, :, 0].reshape(tokens, FEAT)
    cot = x_ref[:, :, 1].reshape(tokens, FEAT)
    acts = act_ref[...].reshape(tokens, QW)
    grads = grad_ref[...].reshape(tokens, QW)

    def tn(left, right):
        return lax.dot_general(left, right, (((0,), (0,)), ((), ())), preferred_element_type=F32)

    for i in range(SUB):
        rows = pl.ds(i * TILE, TILE)
        up = tn(ins[:, i * TILE : (i + 1) * TILE], grads)
        down = tn(acts[:, i * TILE : (i + 1) * TILE], cot)
        for j in range(SUB):
            cols = slice(j * TILE, (j + 1) * TILE)
            gup[rows, cols] = up[:, cols].astype(BF16) * mask_up[i, q * SUB + j].astype(F32).astype(BF16)
            gdown[rows, cols] = down[:, cols].astype(BF16) * mask_down[q * SUB + i, j].astype(F32).astype(BF16)


def weight_grads(x_all, act_all, grad_all, mask_up, mask_down):
    smem = pl.BlockSpec(memory_space=pltpu.SMEM)
    return pl.pallas_call(
        weight_kernel,
        grid=(SIDE,),
        out_shape=[
            jax.ShapeDtypeStruct((FEAT, SIDE * QW), BF16),
            jax.ShapeDtypeStruct((SIDE * QW, FEAT), BF16),
        ],
        in_specs=[
            pl.BlockSpec(x_all.shape, lambda q: (0,) * 5),
            pl.BlockSpec((CHUNKS, SIDE, 1, BLK, QW), lambda q: (0, 0, q, 0, 0)),
            pl.BlockSpec((CHUNKS, 1, SIDE, BLK, QW), lambda q: (0, q, 0, 0, 0)),
            smem,
            smem,
        ],
        out_specs=[pl.BlockSpec((FEAT, QW), lambda q: (0, q)), pl.BlockSpec((QW, FEAT), lambda q: (q, 0))],
        compiler_params=pltpu.CompilerParams(vmem_limit_bytes=40 * 2**20),
    )(x_all, act_all, grad_all, mask_up, mask_down)


def per_device(inputs, w_up, w_down, mask_up, mask_down, cotangent):
    outputs, grad_inputs, x_all, act_all, grad_all = run_block(
        inputs, w_up, w_down, mask_up, mask_down, cotangent
    )
    grad_up, grad_down = weight_grads(x_all, act_all, grad_all, mask_up, mask_down)
    return (outputs.reshape(inputs.shape), grad_inputs.reshape(inputs.shape), grad_up, grad_down)


def solution(mesh):
    in_specs = (
        P("col", "row"),
        P("row", "col"),
        P("col", "row"),
        P("row", "col"),
        P("col", "row"),
        P("col", "row"),
    )
    out_specs = (P("col", "row"), P("col", "row"), P("row", "col"), P("col", "row"))
    return jax.shard_map(
        per_device, mesh=mesh, in_specs=in_specs, out_specs=out_specs, check_vma=False
    )
```

time: 369 us -> 124 us (0.34)
  waiting for transfers between devices: 225 us -> 0 us
  Pallas kernels: 0 us -> 115 us
  local copies, waits for them, and re-layouts: 51.5 us -> 7.84 us
  matrix products: 42.3 us -> 0 us
  blocking collectives: 30.6 us -> 0 us
  between operations: 14.2 us -> 0.67 us
    reduce_scatter x4 -> x0, waiting for transfers between devices: 136 us -> none  [the longest x1 78.4 us: per_device(): lax.psum_scatter(up_part.astype(jnp.bfloat16), 'row', scatter_dimension=0...]
    pallas_call x0 -> x2, Pallas kernels: none -> 115 us  [the longest x1 106 us: run_block(): pl.pallas_call(block_kernel, out_shape=[jax.ShapeDtypeStruct((CHUNKS, ROW...]
    all_gather x2 -> x0, waiting for transfers between devices: 88.4 us -> none  [the longest x1 48 us: per_device(): lax.all_gather(act, 'row', axis=0, tiled=True)]
    dot_general x6 -> x0, matrix products: 42.3 us -> none  [the longest x4 29 us: contract(): lax.dot_general(left, right, (((left_dim,), (right_dim,)), ((), ())), pre...]
    all_gather x2 -> x0, blocking collectives: 30.6 us -> none  [the longest x1 17.2 us: per_device(): lax.all_gather(cotangent, 'col', axis=0, tiled=True)]
    unnamed x24 -> x17, local copies, waits for them, and re-layouts: 36.8 us -> 7.84 us
    mul x4 -> x0, local copies, waits for them, and re-layouts: 14.7 us -> none  [apply_mask(): return (shaped * keep).reshape(weight.shape)]
  transfers between devices with their start and end apart: 6 -> 0, of which waited for: 5 -> 0; matrix products, arithmetic and copies ran while one was open for 20% -> 0% of each run, Pallas kernels for 0% -> 0%
where the time goes in v1:
time: 124 us; the launch traced here: 123 us
  Pallas kernels  115 us (93%)
  local copies, waits for them, and re-layouts  7.84 us (6%)
    pallas_call x1, Pallas kernels, run_block(): pl.pallas_call(block_kernel, out_shape=[jax.ShapeDtypeStruct((CHUNKS, ROW...  106 us
    pallas_call x1, Pallas kernels, weight_grads(): pl.pallas_call(weight_kernel, grid=(SIDE,), out_shape=[jax.ShapeDtypeStru...  8.31 us
    unnamed x17, local copies, waits for them, and re-layouts  7.84 us

profile of v1, /device:TPU:1, one launch (start us, length us, event | category | flops | bytes accessed | tf_op | source)
XLA Modules:
  0.0 123.3 jit_solution(2330826886676623943)
XLA Ops:
  0.6 1.4 %copy.10.mask_down = s32[24,6]{1,0:T(8,128)} copy(s32[24,6]{0,1:T(8,128)} %param.10) | data formatting | bytes 1152 | tf_op args[4]
  2.0 0.0 copy-start.3
  2.0 0.0 copy-start.4
  2.0 106.5 %shard_map.93 = (bf16[4,16,768]{2,1,0:T(8,128)(2,1)}, bf16[4,16,768]{2,1,0:T(8,128)(2,1)}, bf16[4,8,2,16,768]{4,3,2,1,0:T(8,128)(2,1)}, bf16[4,4,4,32,768]{4,3,2,1,0:T(8,128)(2,1)}, bf16[4,4,4,32,768]{4,3,2,1,0:T(8,128)(2,1)}) custom-call(bf16[4,16,768]{2,1,0:T(8,128)(2,1)} %bitcast.4, bf16[768,3072]{1,0:T(8,128)(2,1)} %w_up.1, bf16[3072,768]{1,0:T(8,128)(2,1)} %w_down.1, ...), custom_call_target="tpu_custom_call" | custom-call | tf_op jit(solution)/shard_map/pallas_call | solution.py:261
  108.5 0.0 copy-done.3
  108.5 0.0 copy-done.4
  108.5 0.0 copy-start
  108.5 1.9 %copy-done = bf16[4,4,4,32,768]{4,3,2,1,0:T(8,128)(2,1)S(1)} copy-done((bf16[4,4,4,32,768]{4,3,2,1,0:T(8,128)(2,1)S(1)}, bf16[4,4,4,32,768]{4,3,2,1,0:T(8,128)(2,1)}, u32[]{:S(2)}) %copy-start) | copy-done | bytes 3145752
  110.4 0.0 copy-start.1
  110.4 1.9 %copy-done.1 = bf16[4,4,4,32,768]{4,3,2,1,0:T(8,128)(2,1)S(1)} copy-done((bf16[4,4,4,32,768]{4,3,2,1,0:T(8,128)(2,1)S(1)}, bf16[4,4,4,32,768]{4,3,2,1,0:T(8,128)(2,1)}, u32[]{:S(2)}) %copy-start.1) | copy-done | bytes 3145752
  112.3 0.0 copy-start.2
  112.3 1.4 %copy-done.2 = bf16[4,8,2,16,768]{4,3,2,1,0:T(8,128)(2,1)S(1)} copy-done((bf16[4,8,2,16,768]{4,3,2,1,0:T(8,128)(2,1)S(1)}, bf16[4,8,2,16,768]{4,3,2,1,0:T(8,128)(2,1)}, u32[]{:S(2)}) %copy-start.2) | copy-done | bytes 1572888
  113.7 0.0 copy-start.6
  113.7 0.0 copy-start.5
  113.7 8.3 %shard_map.94 = (bf16[768,3072]{1,0:T(8,128)(2,1)}, bf16[3072,768]{1,0:T(8,128)(2,1)}) custom-call(bf16[4,8,2,16,768]{4,3,2,1,0:T(8,128)(2,1)S(1)} %copy-done.2, bf16[4,4,4,32,768]{4,3,2,1,0:T(8,128)(2,1)S(1)} %copy-done, bf16[4,4,4,32,768]{4,3,2,1,0:T(8,128)(2,1)S(1)} %copy-done.1, s32[6,24]{1,0:T(8,128)S(1)} %copy-done.4, s32[24,6]{1,0:T(8,128)S(1)} %copy-done.3), custom_call_target="tpu_custom_call" | custom-call | tf_op jit(solution)/shard_map/pallas_call | solution.py:331
  122.0 0.0 copy-done.6
  122.0 0.6 copy.14
  122.7 0.0 copy-done.5
  122.7 0.6 copy.15
Async XLA Ops:
  2.0 106.5 %copy-start.3 = (s32[24,6]{1,0:T(8,128)S(1)}, s32[24,6]{1,0:T(8,128)}, u32[]{:S(2)}) copy-start(s32[24,6]{1,0:T(8,128)} %copy.10.mask_down) | copy-start | bytes 1732
  2.0 106.5 %copy-start.4 = (s32[6,24]{1,0:T(8,128)S(1)}, s32[6,24]{1,0:T(8,128)}, u32[]{:S(2)}) copy-start(s32[6,24]{1,0:T(8,128)} %mask_up.3) | copy-start | bytes 1732
  108.5 1.9 %copy-start = (bf16[4,4,4,32,768]{4,3,2,1,0:T(8,128)(2,1)S(1)}, bf16[4,4,4,32,768]{4,3,2,1,0:T(8,128)(2,1)}, u32[]{:S(2)}) copy-start(bf16[4,4,4,32,768]{4,3,2,1,0:T(8,128)(2,1)} %get-tuple-element.14.act_ref) | copy-start | bytes 9437188
  110.4 1.9 %copy-start.1 = (bf16[4,4,4,32,768]{4,3,2,1,0:T(8,128)(2,1)S(1)}, bf16[4,4,4,32,768]{4,3,2,1,0:T(8,128)(2,1)}, u32[]{:S(2)}) copy-start(bf16[4,4,4,32,768]{4,3,2,1,0:T(8,128)(2,1)} %get-tuple-element.15.grad_ref) | copy-start | bytes 9437188
  112.3 1.4 %copy-start.2 = (bf16[4,8,2,16,768]{4,3,2,1,0:T(8,128)(2,1)S(1)}, bf16[4,8,2,16,768]{4,3,2,1,0:T(8,128)(2,1)}, u32[]{:S(2)}) copy-start(bf16[4,8,2,16,768]{4,3,2,1,0:T(8,128)(2,1)} %get-tuple-element.13.x_ref) | copy-start | bytes 4718596
  113.7 8.3 %copy-start.6 = (bf16[4,16,768]{2,1,0:T(8,128)(2,1)S(1)}, bf16[4,16,768]{2,1,0:T(8,128)(2,1)}, u32[]{:S(2)}) copy-start(bf16[4,16,768]{2,1,0:T(8,128)(2,1)} %get-tuple-element.11) | copy-start | bytes 294916
  113.7 9.0 %copy-start.5 = (bf16[4,16,768]{2,1,0:T(8,128)(2,1)S(1)}, bf16[4,16,768]{2,1,0:T(8,128)(2,1)}, u32[]{:S(2)}) copy-start(bf16[4,16,768]{2,1,0:T(8,128)(2,1)} %get-tuple-element.12) | copy-start | bytes 294916

commit v2 on v1

v2 whole, which is shorter than its diff:
```python
import functools

import jax
import jax.numpy as jnp
from jax import lax
from jax.experimental import pallas as pl
from jax.experimental.pallas import tpu as pltpu
from jax.sharding import PartitionSpec as P

MESH = pl.DeviceIdType.MESH
BF16 = jnp.bfloat16
F32 = jnp.float32
SIDE = 4
CHUNKS = 4
COLS = 8
ROWS = 16
TOK = COLS * ROWS
BLK = TOK // SIDE
FEAT = 768
QW = 768
TILE = 128
SUB = FEAT // TILE
S0, S1, S2, S3, S4, S5, S6, S7 = range(8)

ORDER = (
    (0, 0), (0, 1), (1, 0), (0, 2), (1, 1), (0, 3), (2, 0), (1, 2), (2, 1), (1, 3), (3, 0), (2, 2), (3, 1), (2, 3),
    (4, 0), (3, 2), (4, 1), (3, 3), (5, 0), (4, 2), (5, 1), (4, 3), (6, 0), (5, 2), (6, 1), (5, 3), (6, 2), (6, 3),
    (7, 0), (7, 1), (7, 2), (7, 3),
)


def dot(left, right, right_dim):
    return lax.dot_general(left, right, (((1,), (right_dim,)), ((), ())), preferred_element_type=F32)


def block_kernel(
    inputs, w_up, w_down, up_bits, down_bits, cotangent,
    outputs, grad_inputs, xin, xt, act_t, grad,
    up, down, ph, pg, r1h, r1g, r2h, r2g, sh, sg, r3h, r3g, act, po, r7, mask_up, mask_down,
    send, recv, wsem, lsem,
):
    row, col = lax.axis_index("row"), lax.axis_index("col")
    x, y = row // SIDE, lax.rem(row, SIDE)

    def turn(v, by):
        return lax.rem(v + by, SIDE)

    def at_x(by):
        return (turn(x, by) * SIDE + y, col)

    def at_y(by):
        return (x * SIDE + turn(y, by), col)

    def col_of(by):
        return lax.rem(col + by, COLS)

    barrier = pltpu.get_barrier_semaphore()
    partners = [at_x(j) for j in (1, 2, 3)] + [at_y(j) for j in (1, 2, 3)] + [(row, col_of(j)) for j in range(1, COLS)]
    for device in partners:
        pl.semaphore_signal(barrier, inc=1, device_id=device, device_id_type=MESH)

    own = [
        pltpu.make_async_copy(up_bits, mask_up, lsem.at[2]),
        pltpu.make_async_copy(down_bits, mask_down, lsem.at[3]),
        pltpu.make_async_copy(inputs, xin.at[:, col, 0], lsem.at[0]),
        pltpu.make_async_copy(cotangent, xin.at[:, col, 1], lsem.at[1]),
    ]
    for copy in own:
        copy.start()
    loads = []
    for q in range(SIDE):
        loads.append(
            (
                pltpu.make_async_copy(w_up.at[:, pl.ds(q * QW, QW)], up.at[q], wsem.at[0, q]),
                pltpu.make_async_copy(w_down.at[pl.ds(q * QW, QW)], down.at[q], wsem.at[1, q]),
            )
        )
    for pair in loads:
        for copy in pair:
            copy.start()
    for copy in own:
        copy.wait()
    pl.semaphore_wait(barrier, len(partners))

    def ship(c, step, src, dst, device):
        pltpu.make_async_remote_copy(
            src_ref=src,
            dst_ref=dst,
            send_sem=send.at[step],
            recv_sem=recv.at[c, step],
            device_id=device,
            device_id_type=MESH,
        ).start()

    def await_bytes(like, sem):
        pltpu.make_async_copy(like, like, sem).wait()

    def land(c, step):
        like = {S0: r7.at[c], S1: ph.at[c, pl.ds(0, 2)], S2: ph.at[c], S3: ph.at[c, pl.ds(0, 2), pl.ds(0, 3)]}
        like.update({S4: like[S3], S5: like[S2], S6: like[S1], S7: like[S0]})
        await_bytes(like[step], recv.at[c, step])

    def gather(c):
        for j in range(1, COLS):
            ship(c, S0, xin.at[c, col], xin.at[c, col], (row, col_of(j)))

    gather(0)

    def drop_tiles(q, _):
        def one_row(i, _):
            rows = pl.ds(pl.multiple_of(i * TILE, TILE), TILE)
            for j in range(SUB):
                cols = pl.ds(j * TILE, TILE)
                up[q, rows, cols] = up[q, rows, cols] * mask_up[i, q * SUB + j].astype(F32).astype(BF16)
                down[q, rows, cols] = down[q, rows, cols] * mask_down[j, q * SUB + i].astype(F32).astype(BF16)
            return 0

        return lax.fori_loop(0, SUB, one_row, 0)

    for q in range(SIDE):
        for copy in loads[q]:
            copy.wait()
        drop_tiles(q, 0)

    def multiply_in(c):
        land(c, S0)
        if c + 1 < CHUNKS:
            gather(c + 1)

        def ahead(q, _):
            ins = xin[c, :, 0].reshape(TOK, FEAT)
            ph[c, :, q] = dot(ins, up[q], 0).astype(BF16).reshape(SIDE, BLK, QW)
            return 0

        def back(k, _):
            q = turn(y, k)
            cot = xin[c, :, 1].reshape(TOK, FEAT)
            pg[c, q] = dot(cot, down[q], 1).astype(BF16).reshape(SIDE, BLK, QW)
            return 0

        lax.fori_loop(2, 3, back, 0)
        ship(c, S1, pg.at[c, turn(y, 2), pl.ds(0, 2)], r1g.at[c, 0], at_y(1))
        ship(c, S1, pg.at[c, turn(y, 2), pl.ds(2, 2)], r1g.at[c, 1], at_y(3))
        lax.fori_loop(0, 2, ahead, 0)
        ship(c, S1, ph.at[c, turn(x, 2), pl.ds(0, 2)], r1h.at[c, 0], at_x(1))
        lax.fori_loop(2, 4, ahead, 0)
        ship(c, S1, ph.at[c, turn(x, 2), pl.ds(2, 2)], r1h.at[c, 1], at_x(3))
        lax.fori_loop(3, 6, back, 0)

    def add_first(c):
        land(c, S1)

        def half(k, _):
            ph[c, turn(x, 1), k] += r1h[c, 0, k]
            pg[c, turn(y, 1), k] += r1g[c, 0, k]
            ph[c, turn(x, 3), 2 + k] += r1h[c, 1, k]
            pg[c, turn(y, 3), 2 + k] += r1g[c, 1, k]
            return 0

        lax.fori_loop(0, 2, half, 0)
        ship(c, S2, ph.at[c, turn(x, 1)], r2h.at[c, 0], at_x(1))
        ship(c, S2, pg.at[c, turn(y, 1)], r2g.at[c, 0], at_y(1))
        ship(c, S2, ph.at[c, turn(x, 3)], r2h.at[c, 1], at_x(3))
        ship(c, S2, pg.at[c, turn(y, 3)], r2g.at[c, 1], at_y(3))

    def add_second(c):
        land(c, S2)

        def quarter(k, _):
            for own_part, come, total, at in ((ph, r2h, sh, x), (pg, r2g, sg, y)):
                total[c, k] = (
                    own_part[c, at, k].astype(F32) + come[c, 0, k].astype(F32) + come[c, 1, k].astype(F32)
                ).astype(BF16)
            return 0

        lax.fori_loop(0, SIDE, quarter, 0)
        for j in (1, 2, 3):
            ship(c, S3, sh.at[c, turn(y, j)], r3h.at[c, j - 1], at_y(j))
            ship(c, S3, sg.at[c, turn(x, j)], r3g.at[c, j - 1], at_x(j))

    def activate(c):
        land(c, S3)

        def some_rows(i, _):
            rows = pl.ds(pl.multiple_of(i * ROWS, ROWS), ROWS)
            value, slope = sh[c, y, rows].astype(F32), sg[c, x, rows].astype(F32)
            for j in range(3):
                value += r3h[c, j, rows].astype(F32)
                slope += r3g[c, j, rows].astype(F32)
            root = 0.7978845608028654
            square = value * value
            tan = jnp.tanh(root * (value + 0.044715 * (square * value)))
            gate = 0.5 * (1.0 + tan)
            bend = 0.5 * value * (1.0 - tan * tan) * (root * (1.0 + 3.0 * 0.044715 * square))
            act[c, x, y, rows] = (value * gate).astype(BF16)
            grad[c, y, x, rows] = (slope * (gate + bend)).astype(BF16)
            return 0

        lax.fori_loop(0, BLK // ROWS, some_rows, 0)
        for j in (1, 2, 3):
            ship(c, S4, act.at[c, x, y], act.at[c, x, y], at_y(j))
            ship(c, S4, grad.at[c, y, x], grad.at[c, y, x], at_x(j))

    def spread_first(c):
        land(c, S4)
        ship(c, S5, act.at[c, x], act.at[c, x], at_x(1))
        ship(c, S5, grad.at[c, y], grad.at[c, y], at_y(1))
        ship(c, S5, act.at[c, x], act.at[c, x], at_x(3))
        ship(c, S5, grad.at[c, y], grad.at[c, y], at_y(3))

    def spread_second(c):
        land(c, S5)
        low, high = pl.ds(0, 2), pl.ds(2, 2)
        left, right, under, over = turn(x, 3), turn(x, 1), turn(y, 3), turn(y, 1)
        ship(c, S6, act.at[c, left, low], act.at[c, left, low], at_x(1))
        ship(c, S6, grad.at[c, under, low], grad.at[c, under, low], at_y(1))
        ship(c, S6, act.at[c, right, high], act.at[c, right, high], at_x(3))
        ship(c, S6, grad.at[c, over, high], grad.at[c, over, high], at_y(3))

    def multiply_out(c):
        land(c, S6)

        def out_part(n, _):
            cols = pl.ds(pl.multiple_of(n * 256, 256), 256)
            out = jnp.zeros((TOK, 256), F32)
            for q in range(SIDE):
                out += dot(act[c, :, q].reshape(TOK, QW), down[q, :, cols], 0)
            po[c, :, 0, :, cols] = out.astype(BF16).reshape(COLS, ROWS, 256)
            return 0

        def in_part(n, _):
            cols = pl.ds(pl.multiple_of(n * 256, 256), 256)
            out = jnp.zeros((TOK, 256), F32)
            for q in range(SIDE):
                out += dot(grad[c, q].reshape(TOK, QW), up[q, cols], 1)
            po[c, :, 1, :, cols] = out.astype(BF16).reshape(COLS, ROWS, 256)
            return 0

        lax.fori_loop(0, FEAT // 256, out_part, 0)
        for j in range(1, COLS):
            ship(c, S7, po.at[c, col_of(j), 0], r7.at[c, j - 1, 0], (row, col_of(j)))
        lax.fori_loop(0, FEAT // 256, in_part, 0)
        for j in range(1, COLS):
            ship(c, S7, po.at[c, col_of(j), 1], r7.at[c, j - 1, 1], (row, col_of(j)))
        here = slice(c * TOK, (c + 1) * TOK)

        def turned(q, _):
            act_t[q, :, here] = act[c, :, q].reshape(TOK, QW).T
            return 0

        lax.fori_loop(0, SIDE, turned, 0)
        xt[:, here] = xin[c, :, 0].reshape(TOK, FEAT).T

    def finish(c):
        land(c, S7)
        for k, out in enumerate((outputs, grad_inputs)):
            total = po[c, col, k].astype(F32)
            for j in range(COLS - 1):
                total += r7[c, j, k].astype(F32)
            out[c] = total.astype(BF16)

    stages = (multiply_in, add_first, add_second, activate, spread_first, spread_second, multiply_out, finish)
    for stage, c in ORDER:
        stages[stage](c)
    some = ph.at[:, pl.ds(0, 2), pl.ds(0, 3)]
    sent = {S0: r7, S1: ph.at[pl.ds(0, 2)], S2: ph, S3: some, S4: some, S5: ph, S6: ph.at[pl.ds(0, 2)], S7: r7}
    for step, like in sent.items():
        await_bytes(like, send.at[step])


def run_block(inputs, w_up, w_down, mask_up, mask_down, cotangent):
    vmem = pl.BlockSpec(memory_space=pltpu.VMEM)
    hbm = pl.BlockSpec(memory_space=pl.ANY)
    piece = (BLK, QW)

    def buf(*dims):
        return pltpu.VMEM((CHUNKS, *dims), BF16)

    return pl.pallas_call(
        block_kernel,
        out_shape=[
            buf(ROWS, FEAT),
            buf(ROWS, FEAT),
            buf(COLS, 2, ROWS, FEAT),
            pltpu.VMEM((FEAT, CHUNKS * TOK), BF16),
            pltpu.VMEM((SIDE, QW, CHUNKS * TOK), BF16),
            buf(SIDE, SIDE, *piece),
        ],
        in_specs=[hbm] * 6,
        out_specs=[vmem] * 6,
        scratch_shapes=[
            pltpu.VMEM((SIDE, FEAT, QW), BF16),
            pltpu.VMEM((SIDE, QW, FEAT), BF16),
            buf(SIDE, SIDE, *piece),
            buf(SIDE, SIDE, *piece),
            buf(2, 2, *piece),
            buf(2, 2, *piece),
            buf(2, SIDE, *piece),
            buf(2, SIDE, *piece),
            buf(SIDE, *piece),
            buf(SIDE, *piece),
            buf(3, *piece),
            buf(3, *piece),
            buf(SIDE, SIDE, *piece),
            buf(COLS, 2, ROWS, FEAT),
            buf(COLS - 1, 2, ROWS, FEAT),
            pltpu.SMEM((SUB, SIDE * SUB), jnp.int32),
            pltpu.SMEM((SUB, SIDE * SUB), jnp.int32),
            pltpu.SemaphoreType.DMA((8,)),
            pltpu.SemaphoreType.DMA((CHUNKS, 8)),
            pltpu.SemaphoreType.DMA((2, SIDE)),
            pltpu.SemaphoreType.DMA((4,)),
        ],
        compiler_params=pltpu.CompilerParams(
            collective_id=0, has_side_effects=True, vmem_limit_bytes=48 * 2**20
        ),
    )(
        inputs.reshape(CHUNKS, ROWS, FEAT),
        w_up,
        w_down,
        mask_up,
        mask_down.T,
        cotangent.reshape(CHUNKS, ROWS, FEAT),
    )


def weight_kernel(x_all, xt, act_t, grad, out_here, gin_here, mask_up, mask_down, outputs, grad_inputs, gup, gdown):
    step = pl.program_id(0)
    q, half = step // 2, lax.rem(step, 2)
    tokens = CHUNKS * TOK
    width = QW // 2
    first = pl.multiple_of(half * width, width)

    @pl.when(step == 0)
    def _():
        outputs[...] = out_here[...]
        grad_inputs[...] = gin_here[...]

    cot = x_all[:, :, 1].reshape(tokens, FEAT)
    grads = grad[:, q, :, :, pl.ds(first, width)].reshape(tokens, width)

    def up_rows(i, _):
        rows = pl.ds(pl.multiple_of(i * 256, 256), 256)
        up = dot(xt[rows], grads, 0)
        for k in range(2):
            for j in range(SUB // 2):
                cols = slice(j * TILE, (j + 1) * TILE)
                keep = mask_up[2 * i + k, step * (SUB // 2) + j].astype(F32).astype(BF16)
                gup[pl.ds(pl.multiple_of(i * 256 + k * TILE, TILE), TILE), cols] = (
                    up[k * TILE : (k + 1) * TILE, cols].astype(BF16) * keep
                )
        return 0

    lax.fori_loop(0, SUB // 2, up_rows, 0)

    def down_rows(i, _):
        here = pl.multiple_of(i * TILE, TILE)
        down = dot(act_t[q, pl.ds(pl.multiple_of(first + here, TILE), TILE)], cot, 0)
        for j in range(SUB):
            cols = slice(j * TILE, (j + 1) * TILE)
            keep = mask_down[j, step * (SUB // 2) + i].astype(F32).astype(BF16)
            gdown[pl.ds(here, TILE), cols] = down[:, cols].astype(BF16) * keep
        return 0

    lax.fori_loop(0, SUB // 2, down_rows, 0)


def weight_grads(x_all, xt, act_t, grad, outputs, grad_inputs, mask_up, mask_down):
    smem = pl.BlockSpec(memory_space=pltpu.SMEM)
    vmem = pl.BlockSpec(memory_space=pltpu.VMEM)
    width = QW // 2
    whole = pl.BlockSpec(outputs.shape, lambda s: (0, 0, 0))
    return pl.pallas_call(
        weight_kernel,
        grid=(2 * SIDE,),
        out_shape=[
            jax.ShapeDtypeStruct(outputs.shape, BF16),
            jax.ShapeDtypeStruct(outputs.shape, BF16),
            jax.ShapeDtypeStruct((FEAT, SIDE * QW), BF16),
            jax.ShapeDtypeStruct((SIDE * QW, FEAT), BF16),
        ],
        in_specs=[vmem] * 6 + [smem] * 2,
        out_specs=[
            whole,
            whole,
            pl.BlockSpec((FEAT, width), lambda s: (0, s)),
            pl.BlockSpec((width, FEAT), lambda s: (s, 0)),
        ],
        compiler_params=pltpu.CompilerParams(vmem_limit_bytes=24 * 2**20),
    )(x_all, xt, act_t, grad, outputs, grad_inputs, mask_up, mask_down.T)


def per_device(inputs, w_up, w_down, mask_up, mask_down, cotangent):
    kept = run_block(inputs, w_up, w_down, mask_up, mask_down, cotangent)
    outputs, grad_inputs, x_all, xt, act_t, grad = (
        pltpu.with_memory_space_constraint(array, pltpu.VMEM) for array in kept
    )
    outputs, grad_inputs, grad_up, grad_down = weight_grads(
        x_all, xt, act_t, grad, outputs, grad_inputs, mask_up, mask_down
    )
    return (outputs.reshape(inputs.shape), grad_inputs.reshape(inputs.shape), grad_up, grad_down)


def solution(mesh):
    in_specs = (
        P("col", "row"),
        P("row", "col"),
        P("col", "row"),
        P("row", "col"),
        P("col", "row"),
        P("col", "row"),
    )
    out_specs = (P("col", "row"), P("col", "row"), P("row", "col"), P("col", "row"))
    return jax.shard_map(
        per_device, mesh=mesh, in_specs=in_specs, out_specs=out_specs, check_vma=False
    )
```

time: 124 us -> 119 us (0.960)
  local copies, waits for them, and re-layouts: 7.84 us -> 0.01 us
  Pallas kernels: 115 us -> 118 us
    unnamed x17 -> x4, local copies, waits for them, and re-layouts: 7.84 us -> 0.01 us
    pallas_call x2, Pallas kernels: 115 us -> 118 us  [the longest x1 102 us: run_block(): pl.pallas_call(block_kernel, out_shape=[buf(ROWS, FEAT), buf(ROWS, FEAT),...]
where the time goes in v2:
time: 119 us
  Pallas kernels  118 us (99%)
    pallas_call x1, Pallas kernels, run_block(): pl.pallas_call(block_kernel, out_shape=[buf(ROWS, FEAT), buf(ROWS, FEAT),...  102 us
    pallas_call x1, Pallas kernels, weight_grads(): pl.pallas_call(weight_kernel, grid=(2 * SIDE,), out_shape=[jax.ShapeDtype...  16.6 us

profile of v2, /device:TPU:1, one launch (start us, length us, event | category | flops | bytes accessed | tf_op | source)
XLA Modules:
  0.0 118.9 jit_solution(7669509321192641684)
XLA Ops:
  0.6 0.0 copy-start
  0.6 0.0 copy-start.1
  0.7 101.6 %shard_map.93 = (bf16[4,16,768]{2,1,0:T(8,128)(2,1)S(1)}, bf16[4,16,768]{2,1,0:T(8,128)(2,1)S(1)}, bf16[4,8,2,16,768]{4,3,2,1,0:T(8,128)(2,1)S(1)}, bf16[768,512...) custom-call(bf16[4,16,768]{2,1,0:T(8,128)(2,1)} %bitcast.7, ...), custom_call_target="tpu_custom_call" | custom-call | tf_op jit(solution)/shard_map/pallas_call | solution.py:279
  102.2 0.0 copy-done
  102.2 0.0 copy-done.1
  102.3 16.6 %shard_map.94 = (bf16[4,16,768]{2,1,0:T(8,128)(2,1)}, bf16[4,16,768]{2,1,0:T(8,128)(2,1)}, bf16[768,3072]{1,0:T(8,128)(2,1)}, bf16[3072,768]{1,0:T(8,128)(2,1)}) custom-call(bf16[4,8,2,16,768]{4,3,2,1,0:T(8,128)(2,1)S(1)} %get-tuple-element.14.x_all, bf16[768,512]{1,0:T(8,128)(2,1)S(1)} %get-tuple-element.15.xt, ...), custom_call_target="tpu_custom_call" | custom-call | tf_op jit(solution)/shard_map/pallas_call | solution.py:373
Async XLA Ops:
  0.6 101.6 %copy-start = (s32[6,24]{1,0:T(8,128)S(1)}, s32[6,24]{1,0:T(8,128)}, u32[]{:S(2)}) copy-start(s32[6,24]{1,0:T(8,128)} %mask_up.1) | copy-start | bytes 1732
  0.6 101.6 %copy-start.1 = (s32[24,6]{0,1:T(8,128)S(1)}, s32[24,6]{0,1:T(8,128)}, u32[]{:S(2)}) copy-start(s32[24,6]{0,1:T(8,128)} %param.10) | copy-start | bytes 1732

commit v3 on v2

v3 whole, which is shorter than its diff:
```python
import functools

import jax
import jax.numpy as jnp
from jax import lax
from jax.experimental import pallas as pl
from jax.experimental.pallas import tpu as pltpu
from jax.sharding import PartitionSpec as P

MESH = pl.DeviceIdType.MESH
BF16 = jnp.bfloat16
F32 = jnp.float32
SIDE = 4
CHUNKS = 4
HALVES = 2
COLS = 8
ROWS = 16
TOK = COLS * ROWS
BLK = TOK // SIDE
FEAT = 768
QW = 384
TILE = 128
SUB = FEAT // TILE
Z0, K0, S1, S2, S3, S4, S5, S6, S7 = range(9)

ORDER = (
    (0, 0), (0, 1), (0, 2), (0, 3), (1, 0), (0, 4), (1, 1), (0, 5), (1, 2), (0, 6), (1, 3), (0, 7), (2, 0), (1, 4),
    (2, 1), (1, 5), (2, 2), (1, 6), (2, 3), (1, 7), (3, 0), (2, 4), (3, 1), (2, 5), (3, 2), (2, 6), (3, 3), (2, 7),
    (4, 0), (3, 4), (4, 1), (3, 5), (4, 2), (3, 6), (4, 3), (3, 7), (5, 0), (4, 4), (5, 1), (4, 5), (5, 2), (4, 6),
    (5, 3), (4, 7), (6, 0), (5, 4), (6, 1), (5, 5), (6, 2), (5, 6), (6, 3), (5, 7), (6, 4), (6, 5), (6, 6), (6, 7),
    (7, 1), (7, 3), (7, 5), (7, 7),
)


def beside(parts):
    return jnp.concatenate(parts, axis=1)


def dot(left, right, right_dim):
    return lax.dot_general(left, right, (((1,), (right_dim,)), ((), ())), preferred_element_type=F32)


def block_kernel(
    inputs, w_up, w_down, up_bits, down_bits, cotangent,
    outputs, grad_inputs, xin, xt, act_t, grad,
    up, down, ph, pg, r1h, r1g, r2h, r2g, sh, sg, r3h, r3g, act, acc, po, r7, mask_up, mask_down,
    send, recv, recv_col, wsem, lsem,
):
    row, col = lax.axis_index("row"), lax.axis_index("col")
    x, y = row // SIDE, lax.rem(row, SIDE)
    z, core = col // 2, lax.rem(col, 2)

    def turn(v, by):
        return lax.rem(v + by, SIDE)

    def at_x(by):
        return (turn(x, by) * SIDE + y, col)

    def at_y(by):
        return (x * SIDE + turn(y, by), col)

    def col_of(by):
        return lax.rem(col + by, COLS)

    barrier = pltpu.get_barrier_semaphore()
    partners = [at_x(j) for j in (1, 2, 3)] + [at_y(j) for j in (1, 2, 3)] + [(row, col_of(j)) for j in range(1, COLS)]
    for device in partners:
        pl.semaphore_signal(barrier, inc=1, device_id=device, device_id_type=MESH)

    own = [
        pltpu.make_async_copy(up_bits, mask_up, lsem.at[2]),
        pltpu.make_async_copy(down_bits, mask_down, lsem.at[3]),
        pltpu.make_async_copy(inputs, xin.at[:, col, 0], lsem.at[0]),
        pltpu.make_async_copy(cotangent, xin.at[:, col, 1], lsem.at[1]),
    ]
    for copy in own:
        copy.start()
    loads = []
    for b in range(SIDE):
        units = pl.ds(b * FEAT, FEAT)
        loads.append(
            (
                pltpu.make_async_copy(w_up.at[:, units], up.at[b], wsem.at[0, b]),
                pltpu.make_async_copy(w_down.at[units], down.at[b], wsem.at[1, b]),
            )
        )
    for pair in loads:
        for copy in pair:
            copy.start()
    for copy in own:
        copy.wait()
    pl.semaphore_wait(barrier, len(partners))

    def ship(step, landed, src, dst, device):
        pltpu.make_async_remote_copy(
            src_ref=src,
            dst_ref=dst,
            send_sem=send.at[step],
            recv_sem=landed,
            device_id=device,
            device_id_type=MESH,
        ).start()

    def await_bytes(like, sem):
        pltpu.make_async_copy(like, like, sem).wait()

    def land(c, f, step):
        some = ph.at[c, f, pl.ds(0, 2), pl.ds(0, 3)]
        like = {S1: ph.at[c, f, pl.ds(0, 2)], S2: ph.at[c, f], S3: some}
        like.update({S4: some, S5: like[S2], S6: like[S1]})
        await_bytes(like[step], recv.at[c, f, step - S1])

    sibling = (row, 2 * z + 1 - core)

    def gather_z(c):
        for j in (1, 2, 3):
            ship(Z0, recv_col.at[c, 0], xin.at[c, col], xin.at[c, col], (row, 2 * turn(z, j) + core))
        ship(K0, recv_col.at[c, 1], xin.at[c, col], xin.at[c, col], sibling)

    def gather_core(c):
        await_bytes(xin.at[c, pl.ds(0, 3)], recv_col.at[c, 0])
        for j in (1, 2, 3):
            there = 2 * turn(z, j) + core
            ship(K0, recv_col.at[c, 1], xin.at[c, there], xin.at[c, there], sibling)
        if c + 2 < CHUNKS:
            gather_z(c + 2)

    gather_z(0)

    def drop_tiles(q, _):
        def one_row(i, _):
            rows = pl.ds(pl.multiple_of(i * TILE, TILE), TILE)
            for j in range(SUB):
                cols = pl.ds(j * TILE, TILE)
                up[q, rows, cols] = up[q, rows, cols] * mask_up[i, q * SUB + j].astype(F32).astype(BF16)
                down[q, rows, cols] = down[q, rows, cols] * mask_down[j, q * SUB + i].astype(F32).astype(BF16)
            return 0

        return lax.fori_loop(0, SUB, one_row, 0)

    for b in range(SIDE):
        for copy in loads[b]:
            copy.wait()
        drop_tiles(b, 0)
        if b == 1:
            gather_z(1)
    gather_core(0)

    def multiply_in(c, f):
        if f == 0:
            await_bytes(xin.at[c, pl.ds(0, SIDE)], recv_col.at[c, 1])

        def ahead(n, _):
            ins = xin[c, :, 0].reshape(TOK, FEAT)
            wide = dot(ins, up[HALVES * f + n], 0).astype(BF16)
            for k in range(2):
                ph[c, f, :, 2 * n + k] = wide[:, k * QW : (k + 1) * QW].reshape(SIDE, BLK, QW)
            return 0

        def back(k, _):
            n = lax.rem(y // 2 + k, 2)
            cot = xin[c, :, 1].reshape(TOK, FEAT)
            wide = dot(cot, down[HALVES * f + n], 1).astype(BF16)
            for k in range(2):
                pg[c, f, 2 * n + k] = wide[:, k * QW : (k + 1) * QW].reshape(SIDE, BLK, QW)
            return 0

        landed = recv.at[c, f, 0]
        low, high = pl.ds(0, 2), pl.ds(2, 2)
        lax.fori_loop(1, 2, back, 0)
        ship(S1, landed, pg.at[c, f, turn(y, 2), low], r1g.at[c, f, 0], at_y(1))
        ship(S1, landed, pg.at[c, f, turn(y, 2), high], r1g.at[c, f, 1], at_y(3))
        lax.fori_loop(0, 1, ahead, 0)
        ship(S1, landed, ph.at[c, f, turn(x, 2), low], r1h.at[c, f, 0], at_x(1))
        lax.fori_loop(1, 2, ahead, 0)
        ship(S1, landed, ph.at[c, f, turn(x, 2), high], r1h.at[c, f, 1], at_x(3))
        lax.fori_loop(2, 3, back, 0)
        if f == 0 and c + 1 < CHUNKS:
            gather_core(c + 1)
        if f == 1:
            xt[:, c * TOK : (c + 1) * TOK] = xin[c, :, 0].reshape(TOK, FEAT).T

    def add_first(c, f):
        land(c, f, S1)

        def half(k, _):
            ph[c, f, turn(x, 1), k] += r1h[c, f, 0, k]
            pg[c, f, turn(y, 1), k] += r1g[c, f, 0, k]
            ph[c, f, turn(x, 3), 2 + k] += r1h[c, f, 1, k]
            pg[c, f, turn(y, 3), 2 + k] += r1g[c, f, 1, k]
            return 0

        lax.fori_loop(0, 2, half, 0)
        landed = recv.at[c, f, S2 - S1]
        ship(S2, landed, ph.at[c, f, turn(x, 1)], r2h.at[c, f, 0], at_x(1))
        ship(S2, landed, pg.at[c, f, turn(y, 1)], r2g.at[c, f, 0], at_y(1))
        ship(S2, landed, ph.at[c, f, turn(x, 3)], r2h.at[c, f, 1], at_x(3))
        ship(S2, landed, pg.at[c, f, turn(y, 3)], r2g.at[c, f, 1], at_y(3))

    def add_second(c, f):
        land(c, f, S2)

        def quarter(k, _):
            for own_part, come, total, at in ((ph, r2h, sh, x), (pg, r2g, sg, y)):
                total[c, f, k] = (
                    own_part[c, f, at, k].astype(F32) + come[c, f, 0, k].astype(F32) + come[c, f, 1, k].astype(F32)
                ).astype(BF16)
            return 0

        lax.fori_loop(0, SIDE, quarter, 0)
        landed = recv.at[c, f, S3 - S1]
        for j in (1, 2, 3):
            ship(S3, landed, sh.at[c, f, turn(y, j)], r3h.at[c, f, j - 1], at_y(j))
            ship(S3, landed, sg.at[c, f, turn(x, j)], r3g.at[c, f, j - 1], at_x(j))

    def activate(c, f):
        land(c, f, S3)

        def some_rows(i, _):
            rows = pl.ds(pl.multiple_of(i * ROWS, ROWS), ROWS)
            value, slope = sh[c, f, y, rows].astype(F32), sg[c, f, x, rows].astype(F32)
            for j in range(3):
                value += r3h[c, f, j, rows].astype(F32)
                slope += r3g[c, f, j, rows].astype(F32)
            root = 0.7978845608028654
            square = value * value
            tan = jnp.tanh(root * (value + 0.044715 * (square * value)))
            gate = 0.5 * (1.0 + tan)
            bend = 0.5 * value * (1.0 - tan * tan) * (root * (1.0 + 3.0 * 0.044715 * square))
            act[c, f, x, y, rows] = (value * gate).astype(BF16)
            grad[c, f, y, x, rows] = (slope * (gate + bend)).astype(BF16)
            return 0

        lax.fori_loop(0, BLK // ROWS, some_rows, 0)
        landed = recv.at[c, f, S4 - S1]
        for j in (1, 2, 3):
            ship(S4, landed, act.at[c, f, x, y], act.at[c, f, x, y], at_y(j))
            ship(S4, landed, grad.at[c, f, y, x], grad.at[c, f, y, x], at_x(j))

    def spread_first(c, f):
        land(c, f, S4)
        landed = recv.at[c, f, S5 - S1]
        for j in (1, 3):
            ship(S5, landed, act.at[c, f, x], act.at[c, f, x], at_x(j))
            ship(S5, landed, grad.at[c, f, y], grad.at[c, f, y], at_y(j))

    def spread_second(c, f):
        land(c, f, S5)
        low, high = pl.ds(0, 2), pl.ds(2, 2)
        landed = recv.at[c, f, S6 - S1]
        left, right, under, over = turn(x, 3), turn(x, 1), turn(y, 3), turn(y, 1)
        ship(S6, landed, act.at[c, f, left, low], act.at[c, f, left, low], at_x(1))
        ship(S6, landed, grad.at[c, f, under, low], grad.at[c, f, under, low], at_y(1))
        ship(S6, landed, act.at[c, f, right, high], act.at[c, f, right, high], at_x(3))
        ship(S6, landed, grad.at[c, f, over, high], grad.at[c, f, over, high], at_y(3))

    def multiply_out(c, f):
        land(c, f, S6)

        def some_columns(k, n):
            cols = pl.ds(pl.multiple_of(n * 256, 256), 256)
            out = jnp.zeros((TOK, 256), F32)
            for h in range(2):
                quarters = (2 * h, 2 * h + 1)
                if k == 0:
                    left = beside([act[c, f, :, q].reshape(TOK, QW) for q in quarters])
                    out += dot(left, down[HALVES * f + h, :, cols], 0)
                else:
                    left = beside([grad[c, f, q].reshape(TOK, QW) for q in quarters])
                    out += dot(left, up[HALVES * f + h, cols], 1)
            if f == 0:
                acc[c, k, :, cols] = out
            else:
                out += acc[c, k, :, cols]
                po[c, :, k, :, cols] = out.astype(BF16).reshape(COLS, ROWS, 256)

        for k in range(2):

            def some(n, _):
                some_columns(k, n)
                return 0

            lax.fori_loop(0, FEAT // 256, some, 0)
            if f == 1:
                for j in range(1, COLS):
                    there = col_of(j)
                    ship(S7, recv_col.at[c, 2], po.at[c, there, k], r7.at[c, j - 1, k], (row, there))

        def turned(q, _):
            rows = pl.ds(pl.multiple_of(lax.rem(q, 2) * QW, TILE), QW)
            act_t[HALVES * f + q // 2, rows, c * TOK : (c + 1) * TOK] = act[c, f, :, q].reshape(TOK, QW).T
            return 0

        lax.fori_loop(0, SIDE, turned, 0)

    def finish(c, _):
        await_bytes(r7.at[c], recv_col.at[c, 2])
        for k, out in enumerate((outputs, grad_inputs)):
            total = po[c, col, k].astype(F32)
            for j in range(COLS - 1):
                total += r7[c, j, k].astype(F32)
            out[c] = total.astype(BF16)

    stages = (multiply_in, add_first, add_second, activate, spread_first, spread_second, multiply_out, finish)
    for stage, part in ORDER:
        stages[stage](part // HALVES, part % HALVES)
    half, some = ph.at[pl.ds(0, 2)], ph.at[:, :, pl.ds(0, 2), pl.ds(0, 3)]
    sent = {Z0: xin.at[:, pl.ds(0, 3)], K0: xin.at[:, pl.ds(0, 4)], S1: half, S2: ph, S3: some, S4: some, S5: ph, S6: half}
    sent[S7] = r7
    for step, like in sent.items():
        await_bytes(like, send.at[step])


def run_block(inputs, w_up, w_down, mask_up, mask_down, cotangent):
    vmem = pl.BlockSpec(memory_space=pltpu.VMEM)
    hbm = pl.BlockSpec(memory_space=pl.ANY)

    def buf(*dims):
        return pltpu.VMEM((CHUNKS, *dims), BF16)

    def part(*dims):
        return buf(HALVES, *dims, BLK, QW)

    return pl.pallas_call(
        block_kernel,
        out_shape=[
            buf(ROWS, FEAT),
            buf(ROWS, FEAT),
            buf(COLS, 2, ROWS, FEAT),
            pltpu.VMEM((FEAT, CHUNKS * TOK), BF16),
            pltpu.VMEM((SIDE, FEAT, CHUNKS * TOK), BF16),
            part(SIDE, SIDE),
        ],
        in_specs=[hbm] * 6,
        out_specs=[vmem] * 6,
        scratch_shapes=[
            pltpu.VMEM((SIDE, FEAT, FEAT), BF16),
            pltpu.VMEM((SIDE, FEAT, FEAT), BF16),
            part(SIDE, SIDE),
            part(SIDE, SIDE),
            part(2, 2),
            part(2, 2),
            part(2, SIDE),
            part(2, SIDE),
            part(SIDE),
            part(SIDE),
            part(3),
            part(3),
            part(SIDE, SIDE),
            pltpu.VMEM((CHUNKS, 2, TOK, FEAT), F32),
            buf(COLS, 2, ROWS, FEAT),
            buf(COLS - 1, 2, ROWS, FEAT),
            pltpu.SMEM((SUB, SIDE * SUB), jnp.int32),
            pltpu.SMEM((SUB, SIDE * SUB), jnp.int32),
            pltpu.SemaphoreType.DMA((9,)),
            pltpu.SemaphoreType.DMA((CHUNKS, HALVES, 6)),
            pltpu.SemaphoreType.DMA((CHUNKS, 3)),
            pltpu.SemaphoreType.DMA((2, SIDE)),
            pltpu.SemaphoreType.DMA((4,)),
        ],
        compiler_params=pltpu.CompilerParams(
            collective_id=0, has_side_effects=True, vmem_limit_bytes=48 * 2**20
        ),
    )(
        inputs.reshape(CHUNKS, ROWS, FEAT),
        w_up,
        w_down,
        mask_up,
        mask_down.T,
        cotangent.reshape(CHUNKS, ROWS, FEAT),
    )


def weight_kernel(
    x_all, xt, act_t, grad, out_here, gin_here, up_bits, down_bits, outputs, grad_inputs, gup, gdown,
    stage_up, stage_down, mask_up, mask_down, sems,
):
    tokens = CHUNKS * TOK
    bits = [
        pltpu.make_async_copy(up_bits, mask_up, sems.at[0]),
        pltpu.make_async_copy(down_bits, mask_down, sems.at[1]),
    ]
    moves = [
        pltpu.make_async_copy(out_here, outputs, sems.at[2]),
        pltpu.make_async_copy(gin_here, grad_inputs, sems.at[3]),
    ]
    for copy in bits + moves:
        copy.start()
    for b in range(SIDE):
        f, h = b // 2, b % 2
        units = pl.ds(b * FEAT, FEAT)
        grads = beside([grad[:, f, 2 * h + k].reshape(tokens, QW) for k in range(2)])
        for up in (True, False):
            if up:
                wide = dot(xt[...], grads, 0)
            else:
                wide = dot(act_t[b], x_all[:, :, 1].reshape(tokens, FEAT), 0)
            if b == 0 and up:
                for copy in bits:
                    copy.wait()
            stage = stage_up if up else stage_down
            for i in range(SUB):
                for j in range(SUB):
                    keep = mask_up[i, b * SUB + j] if up else mask_down[j, b * SUB + i]
                    rows, cols = slice(i * TILE, (i + 1) * TILE), slice(j * TILE, (j + 1) * TILE)
                    stage[b, rows, cols] = (wide[rows, cols] * keep.astype(F32)).astype(BF16)
            if up:
                copy = pltpu.make_async_copy(stage.at[b], gup.at[:, units], sems.at[4 + 2 * b])
            else:
                copy = pltpu.make_async_copy(stage.at[b], gdown.at[units], sems.at[5 + 2 * b])
            copy.start()
            moves.append(copy)
    for copy in moves:
        copy.wait()


def weight_grads(x_all, xt, act_t, grad, outputs, grad_inputs, mask_up, mask_down):
    vmem = pl.BlockSpec(memory_space=pltpu.VMEM)
    hbm = pl.BlockSpec(memory_space=pl.ANY)
    return pl.pallas_call(
        weight_kernel,
        out_shape=[
            jax.ShapeDtypeStruct(outputs.shape, BF16),
            jax.ShapeDtypeStruct(outputs.shape, BF16),
            jax.ShapeDtypeStruct((FEAT, SIDE * FEAT), BF16),
            jax.ShapeDtypeStruct((SIDE * FEAT, FEAT), BF16),
        ],
        in_specs=[vmem] * 6 + [hbm] * 2,
        out_specs=[hbm] * 4,
        scratch_shapes=[
            pltpu.VMEM((SIDE, FEAT, FEAT), BF16),
            pltpu.VMEM((SIDE, FEAT, FEAT), BF16),
            pltpu.SMEM((SUB, SIDE * SUB), jnp.int32),
            pltpu.SMEM((SUB, SIDE * SUB), jnp.int32),
            pltpu.SemaphoreType.DMA((4 + 2 * SIDE,)),
        ],
        compiler_params=pltpu.CompilerParams(vmem_limit_bytes=24 * 2**20),
    )(x_all, xt, act_t, grad, outputs, grad_inputs, mask_up, mask_down.T)


def per_device(inputs, w_up, w_down, mask_up, mask_down, cotangent):
    kept = run_block(inputs, w_up, w_down, mask_up, mask_down, cotangent)
    outputs, grad_inputs, x_all, xt, act_t, grad = (
        pltpu.with_memory_space_constraint(array, pltpu.VMEM) for array in kept
    )
    outputs, grad_inputs, grad_up, grad_down = weight_grads(
        x_all, xt, act_t, grad, outputs, grad_inputs, mask_up, mask_down
    )
    return (outputs.reshape(inputs.shape), grad_inputs.reshape(inputs.shape), grad_up, grad_down)


def solution(mesh):
    in_specs = (
        P("col", "row"),
        P("row", "col"),
        P("col", "row"),
        P("row", "col"),
        P("col", "row"),
        P("col", "row"),
    )
    out_specs = (P("col", "row"), P("col", "row"), P("row", "col"), P("col", "row"))
    return jax.shard_map(
        per_device, mesh=mesh, in_specs=in_specs, out_specs=out_specs, check_vma=False
    )
```

time: 119 us -> 108 us (0.908)
  Pallas kernels: 118 us -> 107 us
    pallas_call x1, Pallas kernels: 16.6 us -> 6.92 us  [weight_grads(): pl.pallas_call(weight_kernel, out_shape=[jax.ShapeDtypeStruct(outputs.sha...]
where the time goes in v3:
time: 108 us
  Pallas kernels  107 us (99%)
    pallas_call x1, Pallas kernels, run_block(): pl.pallas_call(block_kernel, out_shape=[buf(ROWS, FEAT), buf(ROWS, FEAT),...  101 us
    pallas_call x1, Pallas kernels, weight_grads(): pl.pallas_call(weight_kernel, out_shape=[jax.ShapeDtypeStruct(outputs.sha...  6.92 us

profile of v3, /device:TPU:1, one launch (start us, length us, event | category | flops | bytes accessed | tf_op | source)
XLA Modules:
  0.0 108.3 jit_solution(6053336956525580886)
XLA Ops:
  0.6 0.0 copy-start
  0.6 0.0 copy-start.1
  0.7 100.5 %shard_map.93 = (bf16[4,16,768]{2,1,0:T(8,128)(2,1)S(1)}, bf16[4,16,768]{2,1,0:T(8,128)(2,1)S(1)}, bf16[4,8,2,16,768]{4,3,2,1,0:T(8,128)(2,1)S(1)}, bf16[768,512...) custom-call(bf16[4,16,768]{2,1,0:T(8,128)(2,1)} %bitcast.7, ...), custom_call_target="tpu_custom_call" | custom-call | tf_op jit(solution)/shard_map/pallas_call | solution.py:324
  101.2 0.0 copy-done
  101.2 0.0 copy-done.1
  101.2 6.9 %shard_map.94 = (bf16[4,16,768]{2,1,0:T(8,128)(2,1)}, bf16[4,16,768]{2,1,0:T(8,128)(2,1)}, bf16[768,3072]{1,0:T(8,128)(2,1)}, bf16[3072,768]{1,0:T(8,128)(2,1)}) custom-call(bf16[4,8,2,16,768]{4,3,2,1,0:T(8,128)(2,1)S(1)} %get-tuple-element.14.x_all, bf16[768,512]{1,0:T(8,128)(2,1)S(1)} %get-tuple-element.15.xt, ...), custom_call_target="tpu_custom_call" | custom-call | tf_op jit(solution)/shard_map/pallas_call | solution.py:420
Async XLA Ops:
  0.6 100.5 %copy-start = (s32[6,24]{1,0:T(8,128)S(1)}, s32[6,24]{1,0:T(8,128)}, u32[]{:S(2)}) copy-start(s32[6,24]{1,0:T(8,128)} %up_bits.3) | copy-start | bytes 1732
  0.6 100.5 %copy-start.1 = (s32[24,6]{0,1:T(8,128)S(1)}, s32[24,6]{0,1:T(8,128)}, u32[]{:S(2)}) copy-start(s32[24,6]{0,1:T(8,128)} %param.10) | copy-start | bytes 1732

commit v4 on v3

--- a/solution.py
+++ b/solution.py
@@ -21,14 +21,15 @@
 QW = 384
 TILE = 128
 SUB = FEAT // TILE
-Z0, K0, S1, S2, S3, S4, S5, S6, S7 = range(9)
+Z0, K0, S1, S2, S3, S4, S5, S6, S7, S8, S9 = range(11)
 
 ORDER = (
-    (0, 0), (0, 1), (0, 2), (0, 3), (1, 0), (0, 4), (1, 1), (0, 5), (1, 2), (0, 6), (1, 3), (0, 7), (2, 0), (1, 4),
-    (2, 1), (1, 5), (2, 2), (1, 6), (2, 3), (1, 7), (3, 0), (2, 4), (3, 1), (2, 5), (3, 2), (2, 6), (3, 3), (2, 7),
-    (4, 0), (3, 4), (4, 1), (3, 5), (4, 2), (3, 6), (4, 3), (3, 7), (5, 0), (4, 4), (5, 1), (4, 5), (5, 2), (4, 6),
-    (5, 3), (4, 7), (6, 0), (5, 4), (6, 1), (5, 5), (6, 2), (5, 6), (6, 3), (5, 7), (6, 4), (6, 5), (6, 6), (6, 7),
-    (7, 1), (7, 3), (7, 5), (7, 7),
+    (0, 0), (0, 1), (0, 2), (0, 3), (1, 0), (0, 4), (1, 1), (0, 5), (1, 2), (1, 3), (0, 6), (0, 7), (2, 0), (1, 4),
+    (2, 1), (1, 5), (2, 2), (2, 3), (1, 6), (1, 7), (3, 0), (2, 4), (3, 1), (2, 5), (3, 2), (3, 3), (2, 6), (2, 7),
+    (4, 0), (3, 4), (4, 1), (3, 5), (4, 2), (4, 3), (3, 6), (3, 7), (5, 0), (4, 4), (5, 1), (4, 5), (5, 2), (5, 3),
+    (4, 6), (4, 7), (6, 0), (5, 4), (6, 1), (5, 5), (6, 2), (6, 3), (5, 6), (5, 7), (7, 0), (6, 4), (7, 1), (6, 5),
+    (7, 2), (7, 3), (6, 6), (6, 7), (8, 0), (7, 4), (8, 1), (7, 5), (8, 2), (8, 3), (7, 6), (7, 7), (8, 4), (8, 5),
+    (8, 6), (8, 7), (9, 1), (9, 3), (9, 5), (9, 7),
 )
 
 
@@ -42,8 +43,8 @@
 
 def block_kernel(
     inputs, w_up, w_down, up_bits, down_bits, cotangent,
-    outputs, grad_inputs, xin, xt, act_t, grad,
-    up, down, ph, pg, r1h, r1g, r2h, r2g, sh, sg, r3h, r3g, act, acc, po, r7, mask_up, mask_down,
+    outputs, grad_inputs, up, down,
+    xin, xt, act_t, grad, ph, pg, r1h, r1g, r2h, r2g, sh, sg, r3h, r3g, r4h, r4g, act, acc, po, r9, mask_up, mask_down,
     send, recv, recv_col, wsem, lsem,
 ):
     row, col = lax.axis_index("row"), lax.axis_index("col")
@@ -105,9 +106,8 @@
         pltpu.make_async_copy(like, like, sem).wait()
 
     def land(c, f, step):
-        some = ph.at[c, f, pl.ds(0, 2), pl.ds(0, 3)]
-        like = {S1: ph.at[c, f, pl.ds(0, 2)], S2: ph.at[c, f], S3: some}
-        like.update({S4: some, S5: like[S2], S6: like[S1]})
+        like = {S1: ph.at[c, f, pl.ds(0, 2)], S2: ph.at[c, f], S3: ph.at[c, f, 0, pl.ds(0, 2)], S4: ph.at[c, f, 0]}
+        like.update({S5: like[S4], S6: like[S3], S7: like[S2], S8: like[S1]})
         await_bytes(like[step], recv.at[c, f, step - S1])
 
     sibling = (row, 2 * z + 1 - core)
@@ -209,19 +209,33 @@
 
         lax.fori_loop(0, SIDE, quarter, 0)
         landed = recv.at[c, f, S3 - S1]
-        for j in (1, 2, 3):
-            ship(S3, landed, sh.at[c, f, turn(y, j)], r3h.at[c, f, j - 1], at_y(j))
-            ship(S3, landed, sg.at[c, f, turn(x, j)], r3g.at[c, f, j - 1], at_x(j))
+        low, high = pl.ds(0, ROWS), pl.ds(ROWS, ROWS)
+        ship(S3, landed, sh.at[c, f, turn(y, 2), low], r3h.at[c, f, 0], at_y(1))
+        ship(S3, landed, sg.at[c, f, turn(x, 2), low], r3g.at[c, f, 0], at_x(1))
+        ship(S3, landed, sh.at[c, f, turn(y, 2), high], r3h.at[c, f, 1], at_y(3))
+        ship(S3, landed, sg.at[c, f, turn(x, 2), high], r3g.at[c, f, 1], at_x(3))
+
+    def add_third(c, f):
+        land(c, f, S3)
+        low, high = pl.ds(0, ROWS), pl.ds(ROWS, ROWS)
+        for total, come, at in ((sh, r3h, y), (sg, r3g, x)):
+            total[c, f, turn(at, 1), low] += come[c, f, 0]
+            total[c, f, turn(at, 3), high] += come[c, f, 1]
+        landed = recv.at[c, f, S4 - S1]
+        ship(S4, landed, sh.at[c, f, turn(y, 1)], r4h.at[c, f, 0], at_y(1))
+        ship(S4, landed, sg.at[c, f, turn(x, 1)], r4g.at[c, f, 0], at_x(1))
+        ship(S4, landed, sh.at[c, f, turn(y, 3)], r4h.at[c, f, 1], at_y(3))
+        ship(S4, landed, sg.at[c, f, turn(x, 3)], r4g.at[c, f, 1], at_x(3))
 
     def activate(c, f):
-        land(c, f, S3)
+        land(c, f, S4)
 
         def some_rows(i, _):
             rows = pl.ds(pl.multiple_of(i * ROWS, ROWS), ROWS)
             value, slope = sh[c, f, y, rows].astype(F32), sg[c, f, x, rows].astype(F32)
-            for j in range(3):
-                value += r3h[c, f, j, rows].astype(F32)
-                slope += r3g[c, f, j, rows].astype(F32)
+            for j in range(2):
+                value += r4h[c, f, j, rows].astype(F32)
+                slope += r4g[c, f, j, rows].astype(F32)
             root = 0.7978845608028654
             square = value * value
             tan = jnp.tanh(root * (value + 0.044715 * (square * value)))
@@ -232,59 +246,57 @@
             return 0
 
         lax.fori_loop(0, BLK // ROWS, some_rows, 0)
-        landed = recv.at[c, f, S4 - S1]
-        for j in (1, 2, 3):
-            ship(S4, landed, act.at[c, f, x, y], act.at[c, f, x, y], at_y(j))
-            ship(S4, landed, grad.at[c, f, y, x], grad.at[c, f, y, x], at_x(j))
-
-    def spread_first(c, f):
-        land(c, f, S4)
         landed = recv.at[c, f, S5 - S1]
         for j in (1, 3):
-            ship(S5, landed, act.at[c, f, x], act.at[c, f, x], at_x(j))
-            ship(S5, landed, grad.at[c, f, y], grad.at[c, f, y], at_y(j))
-
-    def spread_second(c, f):
+            ship(S5, landed, act.at[c, f, x, y], act.at[c, f, x, y], at_y(j))
+            ship(S5, landed, grad.at[c, f, y, x], grad.at[c, f, y, x], at_x(j))
+
+    def spread_first(c, f):
         land(c, f, S5)
-        low, high = pl.ds(0, 2), pl.ds(2, 2)
+        low, high = pl.ds(0, ROWS), pl.ds(ROWS, ROWS)
         landed = recv.at[c, f, S6 - S1]
         left, right, under, over = turn(x, 3), turn(x, 1), turn(y, 3), turn(y, 1)
-        ship(S6, landed, act.at[c, f, left, low], act.at[c, f, left, low], at_x(1))
-        ship(S6, landed, grad.at[c, f, under, low], grad.at[c, f, under, low], at_y(1))
-        ship(S6, landed, act.at[c, f, right, high], act.at[c, f, right, high], at_x(3))
-        ship(S6, landed, grad.at[c, f, over, high], grad.at[c, f, over, high], at_y(3))
+        ship(S6, landed, act.at[c, f, x, under, low], act.at[c, f, x, under, low], at_y(1))
+        ship(S6, landed, grad.at[c, f, y, left, low], grad.at[c, f, y, left, low], at_x(1))
+        ship(S6, landed, act.at[c, f, x, over, high], act.at[c, f, x, over, high], at_y(3))
+        ship(S6, landed, grad.at[c, f, y, right, high], grad.at[c, f, y, right, high], at_x(3))
+
+    def spread_second(c, f):
+        land(c, f, S6)
+        landed = recv.at[c, f, S7 - S1]
+        for j in (1, 3):
+            ship(S7, landed, act.at[c, f, x], act.at[c, f, x], at_x(j))
+            ship(S7, landed, grad.at[c, f, y], grad.at[c, f, y], at_y(j))
+
+    def spread_third(c, f):
+        land(c, f, S7)
+        low, high = pl.ds(0, 2), pl.ds(2, 2)
+        landed = recv.at[c, f, S8 - S1]
+        left, right, under, over = turn(x, 3), turn(x, 1), turn(y, 3), turn(y, 1)
+        ship(S8, landed, act.at[c, f, left, low], act.at[c, f, left, low], at_x(1))
+        ship(S8, landed, grad.at[c, f, under, low], grad.at[c, f, under, low], at_y(1))
+        ship(S8, landed, act.at[c, f, right, high], act.at[c, f, right, high], at_x(3))
+        ship(S8, landed, grad.at[c, f, over, high], grad.at[c, f, over, high], at_y(3))
 
     def multiply_out(c, f):
-        land(c, f, S6)
-
-        def some_columns(k, n):
-            cols = pl.ds(pl.multiple_of(n * 256, 256), 256)
-            out = jnp.zeros((TOK, 256), F32)
+        land(c, f, S8)
+        for k in range(2):
+            out = acc[c, k] if f else jnp.zeros((TOK, FEAT), F32)
             for h in range(2):
-                quarters = (2 * h, 2 * h + 1)
+                b, quarters = HALVES * f + h, (2 * h, 2 * h + 1)
                 if k == 0:
                     left = beside([act[c, f, :, q].reshape(TOK, QW) for q in quarters])
-                    out += dot(left, down[HALVES * f + h, :, cols], 0)
+                    out += dot(left, down[b], 0)
                 else:
                     left = beside([grad[c, f, q].reshape(TOK, QW) for q in quarters])
-                    out += dot(left, up[HALVES * f + h, cols], 1)
+                    out += dot(left, up[b], 1)
             if f == 0:
-                acc[c, k, :, cols] = out
+                acc[c, k] = out
             else:
-                out += acc[c, k, :, cols]
-                po[c, :, k, :, cols] = out.astype(BF16).reshape(COLS, ROWS, 256)
-
-        for k in range(2):
-
-            def some(n, _):
-                some_columns(k, n)
-                return 0
-
-            lax.fori_loop(0, FEAT // 256, some, 0)
-            if f == 1:
+                po[c, :, k] = out.astype(BF16).reshape(COLS, ROWS, FEAT)
                 for j in range(1, COLS):
                     there = col_of(j)
-                    ship(S7, recv_col.at[c, 2], po.at[c, there, k], r7.at[c, j - 1, k], (row, there))
+                    ship(S9, recv_col.at[c, 2], po.at[c, there, k], r9.at[c, j - 1, k], (row, there))
 
         def turned(q, _):
             rows = pl.ds(pl.multiple_of(lax.rem(q, 2) * QW, TILE), QW)
@@ -292,21 +304,42 @@
             return 0
 
         lax.fori_loop(0, SIDE, turned, 0)
+        if (c, f) == (CHUNKS - 1, HALVES - 1):
+            lax.fori_loop(0, SIDE, weight_grads, 0)
+
+    def weight_grads(b, _):
+        tokens = CHUNKS * TOK
+        f, h = b // 2, lax.rem(b, 2)
+        grads = beside([grad[:, f, 2 * h + k].reshape(tokens, QW) for k in range(2)])
+        wide = dot(xt[...], grads, 0)
+        for i in range(SUB):
+            for j in range(SUB):
+                rows, cols = slice(i * TILE, (i + 1) * TILE), slice(j * TILE, (j + 1) * TILE)
+                up[b, rows, cols] = (wide[rows, cols] * mask_up[i, b * SUB + j].astype(F32)).astype(BF16)
+        wide = dot(act_t[b], xin[:, :, 1].reshape(tokens, FEAT), 0)
+        for i in range(SUB):
+            for j in range(SUB):
+                rows, cols = slice(i * TILE, (i + 1) * TILE), slice(j * TILE, (j + 1) * TILE)
+                down[b, rows, cols] = (wide[rows, cols] * mask_down[j, b * SUB + i].astype(F32)).astype(BF16)
+        return 0
 
     def finish(c, _):
-        await_bytes(r7.at[c], recv_col.at[c, 2])
+        await_bytes(r9.at[c], recv_col.at[c, 2])
         for k, out in enumerate((outputs, grad_inputs)):
             total = po[c, col, k].astype(F32)
             for j in range(COLS - 1):
-                total += r7[c, j, k].astype(F32)
+                total += r9[c, j, k].astype(F32)
             out[c] = total.astype(BF16)
 
-    stages = (multiply_in, add_first, add_second, activate, spread_first, spread_second, multiply_out, finish)
+    stages = (
+        multiply_in, add_first, add_second, add_third, activate,
+        spread_first, spread_second, spread_third, multiply_out, finish,
+    )
     for stage, part in ORDER:
         stages[stage](part // HALVES, part % HALVES)
-    half, some = ph.at[pl.ds(0, 2)], ph.at[:, :, pl.ds(0, 2), pl.ds(0, 3)]
-    sent = {Z0: xin.at[:, pl.ds(0, 3)], K0: xin.at[:, pl.ds(0, 4)], S1: half, S2: ph, S3: some, S4: some, S5: ph, S6: half}
-    sent[S7] = r7
+    half, quarter, eighth = ph.at[pl.ds(0, 2)], ph.at[0], ph.at[0, 0]
+    sent = {Z0: xin.at[:, pl.ds(0, 3)], K0: xin.at[:, pl.ds(0, 4)], S1: half, S2: ph, S3: eighth, S4: quarter}
+    sent.update({S5: quarter, S6: eighth, S7: ph, S8: half, S9: r9})
     for step, like in sent.items():
         await_bytes(like, send.at[step])
 
@@ -326,16 +359,16 @@
         out_shape=[
             buf(ROWS, FEAT),
             buf(ROWS, FEAT),
+            pltpu.VMEM((SIDE, FEAT, FEAT), BF16),
+            pltpu.VMEM((SIDE, FEAT, FEAT), BF16),
+        ],
+        in_specs=[hbm] * 6,
+        out_specs=[vmem] * 4,
+        scratch_shapes=[
             buf(COLS, 2, ROWS, FEAT),
             pltpu.VMEM((FEAT, CHUNKS * TOK), BF16),
             pltpu.VMEM((SIDE, FEAT, CHUNKS * TOK), BF16),
             part(SIDE, SIDE),
-        ],
-        in_specs=[hbm] * 6,
-        out_specs=[vmem] * 6,
-        scratch_shapes=[
-            pltpu.VMEM((SIDE, FEAT, FEAT), BF16),
-            pltpu.VMEM((SIDE, FEAT, FEAT), BF16),
             part(SIDE, SIDE),
             part(SIDE, SIDE),
             part(2, 2),
@@ -344,16 +377,18 @@
             part(2, SIDE),
             part(SIDE),
             part(SIDE),
-            part(3),
-            part(3),
+            buf(HALVES, 2, ROWS, QW),
+            buf(HALVES, 2, ROWS, QW),
+            part(2),
+            part(2),
             part(SIDE, SIDE),
             pltpu.VMEM((CHUNKS, 2, TOK, FEAT), F32),
             buf(COLS, 2, ROWS, FEAT),
             buf(COLS - 1, 2, ROWS, FEAT),
             pltpu.SMEM((SUB, SIDE * SUB), jnp.int32),
             pltpu.SMEM((SUB, SIDE * SUB), jnp.int32),
-            pltpu.SemaphoreType.DMA((9,)),
-            pltpu.SemaphoreType.DMA((CHUNKS, HALVES, 6)),
+            pltpu.SemaphoreType.DMA((11,)),
+            pltpu.SemaphoreType.DMA((CHUNKS, HALVES, 8)),
             pltpu.SemaphoreType.DMA((CHUNKS, 3)),
             pltpu.SemaphoreType.DMA((2, SIDE)),
             pltpu.SemaphoreType.DMA((4,)),
@@ -371,80 +406,42 @@
     )
 
 
-def weight_kernel(
-    x_all, xt, act_t, grad, out_here, gin_here, up_bits, down_bits, outputs, grad_inputs, gup, gdown,
-    stage_up, stage_down, mask_up, mask_down, sems,
-):
-    tokens = CHUNKS * TOK
-    bits = [
-        pltpu.make_async_copy(up_bits, mask_up, sems.at[0]),
-        pltpu.make_async_copy(down_bits, mask_down, sems.at[1]),
-    ]
-    moves = [
-        pltpu.make_async_copy(out_here, outputs, sems.at[2]),
-        pltpu.make_async_copy(gin_here, grad_inputs, sems.at[3]),
-    ]
-    for copy in bits + moves:
+def store_kernel(out_here, gin_here, up, down, outputs, grad_inputs, gup, gdown, sems):
+    moves = []
+    for b in range(SIDE):
+        units = pl.ds(b * FEAT, FEAT)
+        moves.append(pltpu.make_async_copy(up.at[b], gup.at[:, units], sems.at[2 * b]))
+        moves.append(pltpu.make_async_copy(down.at[b], gdown.at[units], sems.at[2 * b + 1]))
+    moves.append(pltpu.make_async_copy(out_here, outputs, sems.at[2 * SIDE]))
+    moves.append(pltpu.make_async_copy(gin_here, grad_inputs, sems.at[2 * SIDE + 1]))
+    for copy in moves:
         copy.start()
-    for b in range(SIDE):
-        f, h = b // 2, b % 2
-        units = pl.ds(b * FEAT, FEAT)
-        grads = beside([grad[:, f, 2 * h + k].reshape(tokens, QW) for k in range(2)])
-        for up in (True, False):
-            if up:
-                wide = dot(xt[...], grads, 0)
-            else:
-                wide = dot(act_t[b], x_all[:, :, 1].reshape(tokens, FEAT), 0)
-            if b == 0 and up:
-                for copy in bits:
-                    copy.wait()
-            stage = stage_up if up else stage_down
-            for i in range(SUB):
-                for j in range(SUB):
-                    keep = mask_up[i, b * SUB + j] if up else mask_down[j, b * SUB + i]
-                    rows, cols = slice(i * TILE, (i + 1) * TILE), slice(j * TILE, (j + 1) * TILE)
-                    stage[b, rows, cols] = (wide[rows, cols] * keep.astype(F32)).astype(BF16)
-            if up:
-                copy = pltpu.make_async_copy(stage.at[b], gup.at[:, units], sems.at[4 + 2 * b])
-            else:
-                copy = pltpu.make_async_copy(stage.at[b], gdown.at[units], sems.at[5 + 2 * b])
-            copy.start()
-            moves.append(copy)
     for copy in moves:
         copy.wait()
 
 
-def weight_grads(x_all, xt, act_t, grad, outputs, grad_inputs, mask_up, mask_down):
+def store(outputs, grad_inputs, up, down):
     vmem = pl.BlockSpec(memory_space=pltpu.VMEM)
     hbm = pl.BlockSpec(memory_space=pl.ANY)
     return pl.pallas_call(
-        weight_kernel,
+        store_kernel,
         out_shape=[
             jax.ShapeDtypeStruct(outputs.shape, BF16),
             jax.ShapeDtypeStruct(outputs.shape, BF16),
             jax.ShapeDtypeStruct((FEAT, SIDE * FEAT), BF16),
             jax.ShapeDtypeStruct((SIDE * FEAT, FEAT), BF16),
         ],
-        in_specs=[vmem] * 6 + [hbm] * 2,
+        in_specs=[vmem] * 4,
         out_specs=[hbm] * 4,
-        scratch_shapes=[
-            pltpu.VMEM((SIDE, FEAT, FEAT), BF16),
-            pltpu.VMEM((SIDE, FEAT, FEAT), BF16),
-            pltpu.SMEM((SUB, SIDE * SUB), jnp.int32),
-            pltpu.SMEM((SUB, SIDE * SUB), jnp.int32),
-            pltpu.SemaphoreType.DMA((4 + 2 * SIDE,)),
-        ],
-        compiler_params=pltpu.CompilerParams(vmem_limit_bytes=24 * 2**20),
-    )(x_all, xt, act_t, grad, outputs, grad_inputs, mask_up, mask_down.T)
+        scratch_shapes=[pltpu.SemaphoreType.DMA((2 * SIDE + 2,))],
+        compiler_params=pltpu.CompilerParams(vmem_limit_bytes=8 * 2**20),
+    )(outputs, grad_inputs, up, down)
 
 
 def per_device(inputs, w_up, w_down, mask_up, mask_down, cotangent):
     kept = run_block(inputs, w_up, w_down, mask_up, mask_down, cotangent)
-    outputs, grad_inputs, x_all, xt, act_t, grad = (
-        pltpu.with_memory_space_constraint(array, pltpu.VMEM) for array in kept
-    )
-    outputs, grad_inputs, grad_up, grad_down = weight_grads(
-        x_all, xt, act_t, grad, outputs, grad_inputs, mask_up, mask_down
+    outputs, grad_inputs, grad_up, grad_down = store(
+        *(pltpu.with_memory_space_constraint(array, pltpu.VMEM) for array in kept)
     )
     return (outputs.reshape(inputs.shape), grad_inputs.reshape(inputs.shape), grad_up, grad_down)
 

time: 108 us -> 101 us (0.935)
  Pallas kernels: 107 us -> 100 us
    pallas_call x1, Pallas kernels: 101 us -> 96.7 us  [run_block(): pl.pallas_call(block_kernel, out_shape=[buf(ROWS, FEAT), buf(ROWS, FEAT),...]
    pallas_call x1, Pallas kernels: 6.92 us -> 3.73 us  [store(): pl.pallas_call(store_kernel, out_shape=[jax.ShapeDtypeStruct(outputs.shap...]
where the time goes in v4:
time: 101 us
  Pallas kernels  100 us (99%)
    pallas_call x1, Pallas kernels, run_block(): pl.pallas_call(block_kernel, out_shape=[buf(ROWS, FEAT), buf(ROWS, FEAT),...  96.7 us
    pallas_call x1, Pallas kernels, store(): pl.pallas_call(store_kernel, out_shape=[jax.ShapeDtypeStruct(outputs.shap...  3.73 us

profile of v4, /device:TPU:1, one launch (start us, length us, event | category | flops | bytes accessed | tf_op | source)
XLA Modules:
  0.0 101.2 jit_solution(7814274944180584034)
XLA Ops:
  0.6 96.7 %shard_map.93 = (bf16[4,16,768]{2,1,0:T(8,128)(2,1)S(1)}, bf16[4,16,768]{2,1,0:T(8,128)(2,1)S(1)}, bf16[4,768,768]{2,1,0:T(8,128)(2,1)S(1)}, bf16[4,768,768]{2,1,0:T(8,128)(2,1)S(1)}) custom-call(bf16[4,16,768]{2,1,0:T(8,128)(2,1)} %bitcast.5, bf16[768,3072]{1,0:T(8,128)(2,1)} %w_up.1, bf16[3072,768]{1,0:T(8,128)(2,1)} %w_down.1, s32[6,24]{1,0:T(8,128)} %up_bits.1, ...), custom_call_target="tpu_custom_call" | custom-call | tf_op jit(solution)/shard_map/pallas_call | solution.py:357
  97.3 3.7 %shard_map.94 = (bf16[4,16,768]{2,1,0:T(8,128)(2,1)}, bf16[4,16,768]{2,1,0:T(8,128)(2,1)}, bf16[768,3072]{1,0:T(8,128)(2,1)}, bf16[3072,768]{1,0:T(8,128)(2,1)}) custom-call(bf16[4,16,768]{2,1,0:T(8,128)(2,1)S(1)} %get-tuple-element.12.out_here, bf16[4,16,768]{2,1,0:T(8,128)(2,1)S(1)} %get-tuple-element.13.gin_here, ...), custom_call_target="tpu_custom_call" | custom-call | tf_op jit(solution)/shard_map/pallas_call | solution.py:426

commit v5 on v4

--- a/solution.py
+++ b/solution.py
@@ -21,15 +21,16 @@
 QW = 384
 TILE = 128
 SUB = FEAT // TILE
-Z0, K0, S1, S2, S3, S4, S5, S6, S7, S8, S9 = range(11)
+Z0, K0, S1, S2, S3, S4, S5, S6, S7, S8, K9, Z9 = range(12)
 
 ORDER = (
-    (0, 0), (0, 1), (0, 2), (0, 3), (1, 0), (0, 4), (1, 1), (0, 5), (1, 2), (1, 3), (0, 6), (0, 7), (2, 0), (1, 4),
-    (2, 1), (1, 5), (2, 2), (2, 3), (1, 6), (1, 7), (3, 0), (2, 4), (3, 1), (2, 5), (3, 2), (3, 3), (2, 6), (2, 7),
-    (4, 0), (3, 4), (4, 1), (3, 5), (4, 2), (4, 3), (3, 6), (3, 7), (5, 0), (4, 4), (5, 1), (4, 5), (5, 2), (5, 3),
-    (4, 6), (4, 7), (6, 0), (5, 4), (6, 1), (5, 5), (6, 2), (6, 3), (5, 6), (5, 7), (7, 0), (6, 4), (7, 1), (6, 5),
-    (7, 2), (7, 3), (6, 6), (6, 7), (8, 0), (7, 4), (8, 1), (7, 5), (8, 2), (8, 3), (7, 6), (7, 7), (8, 4), (8, 5),
-    (8, 6), (8, 7), (9, 1), (9, 3), (9, 5), (9, 7),
+    (9, 0), (0, 0), (9, 1), (0, 1), (9, 2), (0, 2), (9, 3), (1, 0), (0, 3), (1, 1), (0, 4), (1, 2), (0, 5), (2, 0),
+    (1, 3), (0, 6), (2, 1), (1, 4), (0, 7), (2, 2), (1, 5), (3, 0), (2, 3), (1, 6), (3, 1), (2, 4), (1, 7), (3, 2),
+    (2, 5), (4, 0), (3, 3), (2, 6), (4, 1), (3, 4), (2, 7), (4, 2), (3, 5), (5, 0), (4, 3), (3, 6), (5, 1), (4, 4),
+    (3, 7), (5, 2), (4, 5), (6, 0), (5, 3), (4, 6), (6, 1), (5, 4), (4, 7), (6, 2), (5, 5), (7, 0), (6, 3), (5, 6),
+    (7, 1), (6, 4), (5, 7), (7, 2), (6, 5), (8, 0), (7, 3), (6, 6), (8, 1), (7, 4), (6, 7), (10, 0), (8, 2), (7, 5),
+    (8, 3), (11, 0), (7, 6), (10, 1), (8, 4), (7, 7), (8, 5), (8, 6), (11, 1), (10, 2), (8, 7), (12, 0), (10, 3),
+    (12, 1), (11, 2), (12, 2), (12, 3), (11, 3),
 )
 
 
@@ -44,7 +45,7 @@
 def block_kernel(
     inputs, w_up, w_down, up_bits, down_bits, cotangent,
     outputs, grad_inputs, up, down,
-    xin, xt, act_t, grad, ph, pg, r1h, r1g, r2h, r2g, sh, sg, r3h, r3g, r4h, r4g, act, acc, po, r9, mask_up, mask_down,
+    xin, xt, act_t, grad, ph, pg, r1h, r1g, r2h, r2g, sh, sg, r3h, r3g, r4h, r4g, act, acc, po, rk, r9, mask_up, mask_down,
     send, recv, recv_col, wsem, lsem,
 ):
     row, col = lax.axis_index("row"), lax.axis_index("col")
@@ -60,11 +61,12 @@
     def at_y(by):
         return (x * SIDE + turn(y, by), col)
 
-    def col_of(by):
-        return lax.rem(col + by, COLS)
+    def at_z(by):
+        return (row, 2 * turn(z, by) + core)
 
     barrier = pltpu.get_barrier_semaphore()
-    partners = [at_x(j) for j in (1, 2, 3)] + [at_y(j) for j in (1, 2, 3)] + [(row, col_of(j)) for j in range(1, COLS)]
+    sibling = (row, 2 * z + 1 - core)
+    partners = [at_z(j) for j in (1, 2, 3)] + [sibling, at_x(1), at_x(3), at_y(1), at_y(3)]
     for device in partners:
         pl.semaphore_signal(barrier, inc=1, device_id=device, device_id_type=MESH)
 
@@ -110,11 +112,9 @@
         like.update({S5: like[S4], S6: like[S3], S7: like[S2], S8: like[S1]})
         await_bytes(like[step], recv.at[c, f, step - S1])
 
-    sibling = (row, 2 * z + 1 - core)
-
     def gather_z(c):
         for j in (1, 2, 3):
-            ship(Z0, recv_col.at[c, 0], xin.at[c, col], xin.at[c, col], (row, 2 * turn(z, j) + core))
+            ship(Z0, recv_col.at[c, 0], xin.at[c, col], xin.at[c, col], at_z(j))
         ship(K0, recv_col.at[c, 1], xin.at[c, col], xin.at[c, col], sibling)
 
     def gather_core(c):
@@ -122,8 +122,8 @@
         for j in (1, 2, 3):
             there = 2 * turn(z, j) + core
             ship(K0, recv_col.at[c, 1], xin.at[c, there], xin.at[c, there], sibling)
-        if c + 2 < CHUNKS:
-            gather_z(c + 2)
+        if c == 0:
+            gather_z(3)
 
     gather_z(0)
 
@@ -144,7 +144,7 @@
         drop_tiles(b, 0)
         if b == 1:
             gather_z(1)
-    gather_core(0)
+    gather_z(2)
 
     def multiply_in(c, f):
         if f == 0:
@@ -175,10 +175,6 @@
         lax.fori_loop(1, 2, ahead, 0)
         ship(S1, landed, ph.at[c, f, turn(x, 2), high], r1h.at[c, f, 1], at_x(3))
         lax.fori_loop(2, 3, back, 0)
-        if f == 0 and c + 1 < CHUNKS:
-            gather_core(c + 1)
-        if f == 1:
-            xt[:, c * TOK : (c + 1) * TOK] = xin[c, :, 0].reshape(TOK, FEAT).T
 
     def add_first(c, f):
         land(c, f, S1)
@@ -260,6 +256,8 @@
         ship(S6, landed, grad.at[c, f, y, left, low], grad.at[c, f, y, left, low], at_x(1))
         ship(S6, landed, act.at[c, f, x, over, high], act.at[c, f, x, over, high], at_y(3))
         ship(S6, landed, grad.at[c, f, y, right, high], grad.at[c, f, y, right, high], at_x(3))
+        if f == 0:
+            xt[:, c * TOK : (c + 1) * TOK] = xin[c, :, 0].reshape(TOK, FEAT).T
 
     def spread_second(c, f):
         land(c, f, S6)
@@ -293,23 +291,26 @@
             if f == 0:
                 acc[c, k] = out
             else:
-                po[c, :, k] = out.astype(BF16).reshape(COLS, ROWS, FEAT)
-                for j in range(1, COLS):
-                    there = col_of(j)
-                    ship(S9, recv_col.at[c, 2], po.at[c, there, k], r9.at[c, j - 1, k], (row, there))
-
+                slabs = out.astype(BF16).reshape(SIDE, 2, ROWS, FEAT)
+                for k2 in range(2):
+                    po[c, k, k2] = slabs[:, k2]
+                ship(K9, recv_col.at[c, 2 + k], po.at[c, k, 1 - core], rk.at[c, k], sibling)
+        if c + 1 < CHUNKS:
+            turn_act(c, f)
+
+    def turn_act(c, f):
         def turned(q, _):
             rows = pl.ds(pl.multiple_of(lax.rem(q, 2) * QW, TILE), QW)
             act_t[HALVES * f + q // 2, rows, c * TOK : (c + 1) * TOK] = act[c, f, :, q].reshape(TOK, QW).T
             return 0
 
         lax.fori_loop(0, SIDE, turned, 0)
-        if (c, f) == (CHUNKS - 1, HALVES - 1):
-            lax.fori_loop(0, SIDE, weight_grads, 0)
-
-    def weight_grads(b, _):
+
+    def weight_grads(b):
         tokens = CHUNKS * TOK
-        f, h = b // 2, lax.rem(b, 2)
+        f, h = b // 2, b % 2
+        if h == 0:
+            turn_act(CHUNKS - 1, f)
         grads = beside([grad[:, f, 2 * h + k].reshape(tokens, QW) for k in range(2)])
         wide = dot(xt[...], grads, 0)
         for i in range(SUB):
@@ -321,25 +322,31 @@
             for j in range(SUB):
                 rows, cols = slice(i * TILE, (i + 1) * TILE), slice(j * TILE, (j + 1) * TILE)
                 down[b, rows, cols] = (wide[rows, cols] * mask_down[j, b * SUB + i].astype(F32)).astype(BF16)
-        return 0
-
-    def finish(c, _):
-        await_bytes(r9.at[c], recv_col.at[c, 2])
+
+    def sum_core(c):
+        for k in range(2):
+            await_bytes(rk.at[c, k], recv_col.at[c, 2 + k])
+            po[c, k, core] = (po[c, k, core].astype(F32) + rk[c, k].astype(F32)).astype(BF16)
+            for j in (1, 2, 3):
+                ship(Z9, recv_col.at[c, 4], po.at[c, k, core, turn(z, j)], r9.at[c, j - 1, k], at_z(j))
+
+    def finish(c):
+        await_bytes(r9.at[c], recv_col.at[c, 4])
         for k, out in enumerate((outputs, grad_inputs)):
-            total = po[c, col, k].astype(F32)
-            for j in range(COLS - 1):
+            total = po[c, k, core, z].astype(F32)
+            for j in range(SIDE - 1):
                 total += r9[c, j, k].astype(F32)
             out[c] = total.astype(BF16)
 
     stages = (
-        multiply_in, add_first, add_second, add_third, activate,
-        spread_first, spread_second, spread_third, multiply_out, finish,
+        multiply_in, add_first, add_second, add_third, activate, spread_first, spread_second, spread_third, multiply_out,
+        gather_core, sum_core, finish, weight_grads,
     )
-    for stage, part in ORDER:
-        stages[stage](part // HALVES, part % HALVES)
+    for stage, n in ORDER:
+        stages[stage](*((n // HALVES, n % HALVES) if stage < 9 else (n,)))
     half, quarter, eighth = ph.at[pl.ds(0, 2)], ph.at[0], ph.at[0, 0]
     sent = {Z0: xin.at[:, pl.ds(0, 3)], K0: xin.at[:, pl.ds(0, 4)], S1: half, S2: ph, S3: eighth, S4: quarter}
-    sent.update({S5: quarter, S6: eighth, S7: ph, S8: half, S9: r9})
+    sent.update({S5: quarter, S6: eighth, S7: ph, S8: half, K9: po.at[pl.ds(0, 2)], Z9: r9})
     for step, like in sent.items():
         await_bytes(like, send.at[step])
 
@@ -383,13 +390,14 @@
             part(2),
             part(SIDE, SIDE),
             pltpu.VMEM((CHUNKS, 2, TOK, FEAT), F32),
-            buf(COLS, 2, ROWS, FEAT),
-            buf(COLS - 1, 2, ROWS, FEAT),
+            buf(2, 2, SIDE, ROWS, FEAT),
+            buf(2, SIDE, ROWS, FEAT),
+            buf(SIDE - 1, 2, ROWS, FEAT),
             pltpu.SMEM((SUB, SIDE * SUB), jnp.int32),
             pltpu.SMEM((SUB, SIDE * SUB), jnp.int32),
-            pltpu.SemaphoreType.DMA((11,)),
+            pltpu.SemaphoreType.DMA((12,)),
             pltpu.SemaphoreType.DMA((CHUNKS, HALVES, 8)),
-            pltpu.SemaphoreType.DMA((CHUNKS, 3)),
+            pltpu.SemaphoreType.DMA((CHUNKS, 5)),
             pltpu.SemaphoreType.DMA((2, SIDE)),
             pltpu.SemaphoreType.DMA((4,)),
         ],

time: 101 us -> 99.6 us (0.986)
  Pallas kernels: 100 us -> 98.6 us
    pallas_call x1, Pallas kernels: 96.7 us -> 94.9 us  [run_block(): pl.pallas_call(block_kernel, out_shape=[buf(ROWS, FEAT), buf(ROWS, FEAT),...]
where the time goes in v5:
time: 99.6 us; the launch traced here: 99.4 us
  Pallas kernels  98.6 us (99%)
    pallas_call x1, Pallas kernels, run_block(): pl.pallas_call(block_kernel, out_shape=[buf(ROWS, FEAT), buf(ROWS, FEAT),...  94.9 us
    pallas_call x1, Pallas kernels, store(): pl.pallas_call(store_kernel, out_shape=[jax.ShapeDtypeStruct(outputs.shap...  3.73 us

profile of v5, /device:TPU:1, one launch (start us, length us, event | category | flops | bytes accessed | tf_op | source)
XLA Modules:
  0.0 99.4 jit_solution(13465072270871417226)
XLA Ops:
  0.6 94.9 %shard_map.93 = (bf16[4,16,768]{2,1,0:T(8,128)(2,1)S(1)}, bf16[4,16,768]{2,1,0:T(8,128)(2,1)S(1)}, bf16[4,768,768]{2,1,0:T(8,128)(2,1)S(1)}, bf16[4,768,768]{2,1,0:T(8,128)(2,1)S(1)}) custom-call(bf16[4,16,768]{2,1,0:T(8,128)(2,1)} %bitcast.5, bf16[768,3072]{1,0:T(8,128)(2,1)} %w_up.1, bf16[3072,768]{1,0:T(8,128)(2,1)} %w_down.1, s32[6,24]{1,0:T(8,128)} %up_bits.1, ...), custom_call_target="tpu_custom_call" | custom-call | tf_op jit(solution)/shard_map/pallas_call | solution.py:364
  95.5 3.7 %shard_map.94 = (bf16[4,16,768]{2,1,0:T(8,128)(2,1)}, bf16[4,16,768]{2,1,0:T(8,128)(2,1)}, bf16[768,3072]{1,0:T(8,128)(2,1)}, bf16[3072,768]{1,0:T(8,128)(2,1)}) custom-call(bf16[4,16,768]{2,1,0:T(8,128)(2,1)S(1)} %get-tuple-element.12.out_here, bf16[4,16,768]{2,1,0:T(8,128)(2,1)S(1)} %get-tuple-element.13.gin_here, ...), custom_call_target="tpu_custom_call" | custom-call | tf_op jit(solution)/shard_map/pallas_call | solution.py:434

commit v6 on v5

--- a/solution.py
+++ b/solution.py
@@ -418,10 +418,13 @@
     moves = []
     for b in range(SIDE):
         units = pl.ds(b * FEAT, FEAT)
-        moves.append(pltpu.make_async_copy(up.at[b], gup.at[:, units], sems.at[2 * b]))
-        moves.append(pltpu.make_async_copy(down.at[b], gdown.at[units], sems.at[2 * b + 1]))
-    moves.append(pltpu.make_async_copy(out_here, outputs, sems.at[2 * SIDE]))
-    moves.append(pltpu.make_async_copy(gin_here, grad_inputs, sems.at[2 * SIDE + 1]))
+        for k in range(2):
+            rows = pl.ds(k * QW, QW)
+            there = pl.ds(b * FEAT + k * QW, QW)
+            moves.append(pltpu.make_async_copy(up.at[b, rows], gup.at[rows, units], sems.at[4 * b + k]))
+            moves.append(pltpu.make_async_copy(down.at[b, rows], gdown.at[there], sems.at[4 * b + 2 + k]))
+    moves.append(pltpu.make_async_copy(out_here, outputs, sems.at[4 * SIDE]))
+    moves.append(pltpu.make_async_copy(gin_here, grad_inputs, sems.at[4 * SIDE + 1]))
     for copy in moves:
         copy.start()
     for copy in moves:
@@ -441,7 +444,7 @@
         ],
         in_specs=[vmem] * 4,
         out_specs=[hbm] * 4,
-        scratch_shapes=[pltpu.SemaphoreType.DMA((2 * SIDE + 2,))],
+        scratch_shapes=[pltpu.SemaphoreType.DMA((4 * SIDE + 2,))],
         compiler_params=pltpu.CompilerParams(vmem_limit_bytes=8 * 2**20),
     )(outputs, grad_inputs, up, down)
 

time: 99.6 us -> 99.6 us (level)
  no operation moved by 1% of the time
where the time goes in v6:
time: 99.6 us; the launch traced here: 99.5 us
  Pallas kernels  98.7 us (99%)
    pallas_call x1, Pallas kernels, run_block(): pl.pallas_call(block_kernel, out_shape=[buf(ROWS, FEAT), buf(ROWS, FEAT),...  94.9 us
    pallas_call x1, Pallas kernels, store(): pl.pallas_call(store_kernel, out_shape=[jax.ShapeDtypeStruct(outputs.shap...  3.8 us

profile of v6, /device:TPU:1, one launch (start us, length us, event | category | flops | bytes accessed | tf_op | source)
XLA Modules:
  0.0 99.5 jit_solution(17855078812681830780)
XLA Ops:
  0.6 94.9 %shard_map.93 = (bf16[4,16,768]{2,1,0:T(8,128)(2,1)S(1)}, bf16[4,16,768]{2,1,0:T(8,128)(2,1)S(1)}, bf16[4,768,768]{2,1,0:T(8,128)(2,1)S(1)}, bf16[4,768,768]{2,1,0:T(8,128)(2,1)S(1)}) custom-call(bf16[4,16,768]{2,1,0:T(8,128)(2,1)} %bitcast.5, bf16[768,3072]{1,0:T(8,128)(2,1)} %w_up.1, bf16[3072,768]{1,0:T(8,128)(2,1)} %w_down.1, s32[6,24]{1,0:T(8,128)} %up_bits.1, ...), custom_call_target="tpu_custom_call" | custom-call | tf_op jit(solution)/shard_map/pallas_call | solution.py:364
  95.5 3.8 %shard_map.94 = (bf16[4,16,768]{2,1,0:T(8,128)(2,1)}, bf16[4,16,768]{2,1,0:T(8,128)(2,1)}, bf16[768,3072]{1,0:T(8,128)(2,1)}, bf16[3072,768]{1,0:T(8,128)(2,1)}) custom-call(bf16[4,16,768]{2,1,0:T(8,128)(2,1)S(1)} %get-tuple-element.12.out_here, bf16[4,16,768]{2,1,0:T(8,128)(2,1)S(1)} %get-tuple-element.13.gin_here, ...), custom_call_target="tpu_custom_call" | custom-call | tf_op jit(solution)/shard_map/pallas_call | solution.py:437
